TPU v7x, 128 devices: a whole 4x4x4 slice. The times are simulated.
128 devices in a mesh: dp: 8 (over x, y_hi), ctx: 16 (over z, y_lo, core).
Axes of the slice: x: 4, y: 4 (y_hi: 2, y_lo: 2; y = y_hi * 2 + y_lo), z: 4, core: 2. Of those that a mesh axis runs over, the one named last changes fastest.
Arguments:
- q_raw: bfloat16 [8, 8192, 1024], P('dp', 'ctx'), may hold values from -6 to 6
- k_raw: bfloat16 [8, 8192, 128], P('dp', 'ctx'), may hold values from -6 to 6
- values: bfloat16 [8, 8192, 128], P('dp', 'ctx'), may hold values from -6 to 6
- d_out: bfloat16 [8, 8192, 1024], P('dp', 'ctx'), may hold values from -160 to 160
- q_gain: float32 [128], replicated, may hold values from 0.5 to 7
- k_gain: float32 [128], replicated, may hold values from 0.5 to 7
- resp_len: int32 [8, 8], P('dp'), may hold values from 1 to 1408, as said below
- block_parent: int32 [8, 64], P('dp'), may hold values from -1 to 62, as said below
- block_from: int32 [8, 64], P('dp', 'ctx'), may hold values from 0 to 63, as said below
Outputs:
- grad_q: bfloat16 [8, 8192, 1024], P('dp', 'ctx')
- grad_k: bfloat16 [8, 8192, 128], P('dp', 'ctx')
- grad_v: bfloat16 [8, 8192, 128], P('dp', 'ctx')
- q_gain_grad: float32 [128], replicated
- k_gain_grad: float32 [128], replicated
Inputs may be any that keep to these rules, and one draw needn't show every extreme that they name: The responses of a tree follow the prompt's 16 blocks in order and fill its 64 blocks exactly; response r takes ceil(resp_len[t, r] / 128) blocks; the last response of each tree has exactly 11 blocks, all tokens live, and none has more. `block_parent`: block 0 has parent -1; prompt block b > 0 has parent b - 1; the first block of a response has parent 16 - 1 and its other blocks the block before. No block has more than 26 ancestors. Each block number appears once in a tree, and block_from[t, j] // 4 == j // 4.
All inputs are finite; a program needn't handle non-finite values.
Results may differ from a plain program's by a relative error of at most 0.035.
The roundings to bfloat16 on the way count: a program that leaves them out, or rounds other values in their place, can miss the bound.
Values may be sent and summed in bfloat16 or wider, within the bound.
A program may use at most 128 MiB of HBM per device.

v0:
```python
import math

import jax
import jax.numpy as jnp
from jax import lax
from jax.sharding import PartitionSpec as P

BLK = 128


def contract_last(left, right):
    return lax.dot_general(
        left, right, (((1,), (1,)), ((), ())), preferred_element_type=jnp.float32
    )


def contract_first(left, right):
    return lax.dot_general(
        left, right, (((0,), (0,)), ((), ())), preferred_element_type=jnp.float32
    )


def live_tokens(resp_len, block_total, prompt_blocks):
    counts = (resp_len + BLK - 1) // BLK
    block_ends = prompt_blocks + jnp.cumsum(counts, dtype=jnp.int32)
    block_starts = block_ends - counts
    blocks = jnp.arange(block_total, dtype=jnp.int32)
    inside = (blocks[:, None] >= block_starts[None, :]) & (blocks[:, None] < block_ends[None, :])
    first_block = jnp.sum(jnp.where(inside, block_starts[None, :], 0), axis=1)
    length = jnp.sum(jnp.where(inside, resp_len[None, :], 0), axis=1)
    offset = (blocks - first_block)[:, None] * BLK + jnp.arange(BLK, dtype=jnp.int32)[None, :]
    alive_mask = (blocks[:, None] < prompt_blocks) | (offset < length[:, None])
    return alive_mask


def ancestors(block_parent, chain_depth):
    anchor = jnp.arange(block_parent.shape[0], dtype=jnp.int32)

    def climb(current, unused):
        parent_now = jnp.where(current >= 0, block_parent[jnp.maximum(current, 0)], -1)
        return (parent_now, parent_now)

    unused_last, climbed = lax.scan(climb, anchor, None, length=chain_depth - 1)
    return jnp.concatenate([anchor[None, :], climbed], axis=0).T


def normalize(raw, gain):
    values_f = raw.astype(jnp.float32)
    inverse_rms = lax.rsqrt(jnp.mean(values_f * values_f, axis=-1, keepdims=True) + 1e-06)
    unit_vec = values_f * inverse_rms
    return (unit_vec, inverse_rms, (unit_vec * gain).astype(jnp.bfloat16))


def unnormalize(gradient, unit_vec, inverse_rms, gain):
    scaled = gradient * gain
    return inverse_rms * (scaled - unit_vec * jnp.mean(scaled * unit_vec, axis=-1, keepdims=True))


def attend(q_blk, d_blk, keys_win, vals_win, allowed, score_scale):
    scores = contract_last(q_blk, keys_win) * score_scale
    scores = jnp.where(allowed, scores, -jnp.inf)
    row_top = jnp.max(scores, axis=1, keepdims=True)
    weights = jnp.exp(scores - row_top)
    chances = weights / jnp.sum(weights, axis=1, keepdims=True)
    chances_b = chances.astype(jnp.bfloat16)
    attn_out = jnp.dot(chances_b, vals_win, preferred_element_type=jnp.float32)
    row_delta = jnp.sum(d_blk.astype(jnp.float32) * attn_out, axis=1, keepdims=True)
    d_chances = contract_last(d_blk, vals_win)
    d_scores = (chances * (d_chances - row_delta)).astype(jnp.bfloat16)
    query_grad = jnp.dot(d_scores, keys_win, preferred_element_type=jnp.float32) * score_scale
    key_grad = contract_first(d_scores, q_blk) * score_scale
    value_grad = contract_first(chances_b, d_blk)
    return (query_grad, key_grad, value_grad)


def block_pass(key_store, store_ids, ancestry, live_blocks, q_blocks, d_blocks, score_scale):
    head_size = key_store.shape[2]
    store_blocks = key_store.shape[1] // BLK
    head_rows = q_blocks.shape[1]
    head_count = head_rows // BLK
    chain_depth = ancestry.shape[1]
    width = chain_depth * BLK
    tree_blocks = live_blocks.shape[0]
    store_flat = key_store.reshape(2, store_blocks, BLK * head_size)
    live_table = live_blocks.astype(jnp.float32)
    arange_b = jnp.arange(BLK, dtype=jnp.int32)
    store_iota = jnp.arange(store_blocks, dtype=jnp.int32)
    tree_iota = jnp.arange(tree_blocks, dtype=jnp.int32)
    later_block = jnp.arange(chain_depth, dtype=jnp.int32)[None, :, None] > 0
    earlier_col = arange_b[None, None, :] <= arange_b[:, None, None]

    def step(gradients, inputs):
        q_blk, d_blk, block_ids, links = inputs
        picker = (block_ids[:, None] == store_iota[None, :]) & (links >= 0)[:, None]
        window = jnp.einsum(
            "dn,snx->sdx",
            picker.astype(jnp.bfloat16),
            store_flat,
            preferred_element_type=jnp.float32,
        ).astype(jnp.bfloat16)
        window = window.reshape(2, width, head_size)
        chooser = (links[:, None] == tree_iota[None, :]).astype(jnp.float32)
        visible = jnp.dot(chooser, live_table, preferred_element_type=jnp.float32) > 0.5
        allowed = visible[None, :, :] & (later_block | earlier_col)
        allowed = jnp.broadcast_to(
            allowed.reshape(BLK, 1, width), (BLK, head_count, width)
        ).reshape(head_rows, width)
        query_grad, key_grad, value_grad = attend(
            q_blk, d_blk, window[0], window[1], allowed, score_scale
        )
        block_grads = jnp.stack([key_grad, value_grad]).reshape(2, chain_depth, BLK * head_size)
        gradients = gradients + jnp.einsum(
            "dn,sdx->snx",
            picker.astype(jnp.float32),
            block_grads,
            precision=lax.Precision.HIGHEST,
            preferred_element_type=jnp.float32,
        )
        return (gradients, query_grad)

    start_grads = jnp.zeros((2, store_blocks, BLK * head_size), jnp.float32)
    gradients, query_grad = lax.scan(step, start_grads, (q_blocks, d_blocks, store_ids, ancestry))
    return (gradients.reshape(2, store_blocks * BLK, head_size), query_grad)


def body(q_raw, k_raw, values, d_out, q_gain, k_gain, resp_len, block_parent, block_from):
    tok_rows = k_raw.shape[1]
    head_size = k_raw.shape[2]
    head_count = q_raw.shape[2] // head_size
    block_total = block_parent.shape[1]
    responses = resp_len.shape[1]
    blocks_mine = tok_rows // BLK
    base_blocks = 3 * block_total // (4 * responses)
    prompt_blocks = block_total - responses * base_blocks
    chain_depth = prompt_blocks + 2 * base_blocks - 1
    score_scale = 1.0 / math.sqrt(head_size)
    ctx_index = lax.axis_index("ctx")
    first_block = ctx_index * blocks_mine
    live_blocks = live_tokens(resp_len[0], block_total, prompt_blocks)
    ancestry = lax.dynamic_slice_in_dim(
        ancestors(block_parent[0], chain_depth), first_block, blocks_mine, 0
    )
    live_mine = lax.dynamic_slice_in_dim(live_blocks, first_block, blocks_mine, 0).reshape(-1)
    d_blocks = d_out[0].reshape(blocks_mine, BLK * head_count * head_size)
    local_from = block_from[0] - first_block
    placing = (local_from[:, None] == jnp.arange(blocks_mine, dtype=jnp.int32)[None, :]).astype(
        jnp.bfloat16
    )
    d_local = (
        contract_first(placing, d_blocks)
        .astype(jnp.bfloat16)
        .reshape(tok_rows, head_count * head_size)
    )
    d_mask = d_local * live_mine[:, None].astype(jnp.bfloat16)
    q_unit, q_inverse, q_norm = normalize(q_raw[0].reshape(tok_rows, head_count, head_size), q_gain)
    k_unit, k_inverse, k_norm = normalize(k_raw[0], k_gain)
    local_pair = jnp.stack([k_norm, values[0]])
    key_store = lax.all_gather(local_pair, "ctx", axis=1, tiled=True)
    store_ids = jnp.maximum(ancestry, 0)
    gradients, query_grad = block_pass(
        key_store,
        store_ids,
        ancestry,
        live_blocks,
        q_norm.reshape(blocks_mine, BLK * head_count, head_size),
        d_mask.reshape(blocks_mine, BLK * head_count, head_size),
        score_scale,
    )
    d_qnorm = query_grad.reshape(tok_rows, head_count, head_size)
    q_part = jnp.sum(d_qnorm * q_unit, axis=(0, 1))
    own_grads = lax.psum_scatter(gradients, "ctx", scatter_dimension=1, tiled=True)
    k_part = jnp.sum(own_grads[0] * k_unit, axis=0)
    q_total, k_total = lax.psum((q_part, k_part), ("dp", "ctx"))
    grad_q = (
        unnormalize(d_qnorm, q_unit, q_inverse, q_gain)
        .astype(jnp.bfloat16)
        .reshape(tok_rows, head_count * head_size)
    )
    grad_k = unnormalize(own_grads[0], k_unit, k_inverse, k_gain).astype(jnp.bfloat16)
    grad_v = own_grads[1].astype(jnp.bfloat16)
    return (grad_q[None], grad_k[None], grad_v[None], q_total, k_total)


def solution(mesh):
    placed = (
        P("dp", "ctx", None),
        P("dp", "ctx", None),
        P("dp", "ctx", None),
        P("dp", "ctx", None),
        P(),
        P(),
        P("dp", None),
        P("dp", None),
        P("dp", "ctx"),
    )
    return jax.shard_map(
        body,
        mesh=mesh,
        in_specs=placed,
        out_specs=(P("dp", "ctx", None), P("dp", "ctx", None), P("dp", "ctx", None), P(), P()),
        check_vma=False,
    )
```

profile of v0, /device:TPU:1, one launch (start us, length us, event | category | flops | bytes accessed | tf_op | source)
XLA Modules:
  0.0 546.9 jit_solution(3690422375770680857)
XLA Ops:
  10.0 1.6 pad_maximum_fusion
  11.7 39.4 %while.27 = (s32[]{:T(128)}, s32[64]{0:T(128)S(1)}, s32[26,64]{1,0:T(8,128)S(1)}, s32[64]{0:T(128)}, s32[]{:T(128)}, /*index=5*/s32[]{:T(128)}) while((s32[]{:T(128)}, s32[64]{0:T(128)S(1)}, s32[26,64]{1,0:T(8,128)S(1)}, s32[64]{0:T(128)}, s32[]{:T(128)}, /*index=5*/s32[]{:T(128)}) %tuple.68), condition=%wide.region_5.6_spmd, body=%wide.region_4.5_spmd.sunk | while | flops 1218 | bytes 6985 | solution.py:43
  58.4 1.8 copy.22
  60.2 2.9 reduce_sum.92
  66.9 7.3 %reshape.341 = bf16[2,64,16384]{2,1,0:T(8,128)(2,1)} reshape(bf16[2,8192,128]{2,1,0:T(8,128)(2,1)} %all-gather.2.cloned.1.call-done) | data formatting | bytes 8388608 | tf_op jit(solution)/shard_map/reshape | solution.py:84
  74.2 286.5 %while.28 = (s32[]{:T(128)}, f32[2,64,16384]{2,1,0:T(8,128)}, f32[4,1024,128]{2,1,0:T(8,128)}, s32[4,27]{1,0:T(4,128)S(1)}, bf16[4,1024,128]{2,1,0:T(8,128)(2,1)...) while((s32[]{:T(128)}, f32[2,64,16384]{2,1,0:T(8,128)}, ...), condition=%wide.region_11.12_spmd.clone.clone, body=%wide.region_7.11_spmd.clone.clone.sunk | while | flops 6293480448 | bytes 257995504 | solution.py:122
  74.2 2.9 fusion.144
  81.3 5.0 fusion.146
  86.3 4.8 fusion.147
  91.1 7.3 %fusion.148 = f32[1024,3456]{1,0:T(8,128)} fusion(f32[1024,3456]{1,0:T(8,128)S(1)} %get-tuple-element.348, f32[1024]{0:T(1024)S(1)} %fusion.147, f32[1024]{0:T(1024)S(1)} %get-tuple-element.349, pred[128,3456]{1,0:T(8,128)(4,1)S(1)} %copy.27), kind=kLoop, calls=%fused_computation.16.clone.1 | loop fusion | flops 14155776 | bytes 28762112 | tf_op jit(solution)/shard_map/while/body/eval_jaxpr/div | solution.py:64
  99.0 7.6 %fusion.150 = f32[1024]{0:T(1024)S(1)} fusion(bf16[3456,128]{1,0:T(8,128)(2,1)S(1)} %squeeze.46, f32[1024,3456]{1,0:T(8,128)} %fusion.148, bf16[4,1024,128]{1,2,0:T(8,128)(2,1)S(1)} %copy-done.2, s32[]{:T(128)} %get-tuple-element.382), kind=kOutput, calls=%fused_computation.32.clone.1 | convolution fusion | flops 909900800 | bytes 15306756 | tf_op jit(solution)/shard_map/while/body/eval_jaxpr/dot_general | solution.py:66
  108.0 5.1 multiply_convert_fusion.4
  113.1 5.1 convolution_multiply_fusion.3
  118.2 1.6 stack.26
  119.8 8.3 %fusion.149 = f32[3456,128]{1,0:T(8,128)} fusion(f32[1024,3456]{1,0:T(8,128)} %fusion.148, bf16[4,1024,128]{1,2,0:T(8,128)(2,1)S(1)} %copy-done.2, s32[]{:T(128)} %get-tuple-element.382), kind=kOutput, calls=%fused_computation.22.clone.1 | convolution fusion | flops 909508608 | bytes 16187396 | tf_op jit(solution)/shard_map/while/body/eval_jaxpr/dot_general | solution.py:18
  128.1 2.9 stack.25
  131.0 10.1 %fusion.151 = f32[2,64,16384]{2,1,0:T(8,128)} fusion(f32[2,64,16384]{2,1,0:T(8,128)} %get-tuple-element.383, f32[1,27,16384]{2,1,0:T(8,128)} %stack.25, f32[1,27,16384]{2,1,0:T(8,128)} %stack.26, pred[]{:T(512)S(6)} %compare.15, s32[27]{0:T(128)S(1)} %fusion.143, pred[27]{0:T(512)(128)(4,1)S(1)} %get-tuple-element.346), kind=kOutput, calls=%fused_computation.9.clone.1 | convolution fusion | flops 684559744 | bytes 20316296 | tf_op jit(solution)/shard_map/while/body/eval_jaxpr/dn,sdx->snx/dot_general | solution.py:112
  141.2 2.8 fusion.152
  144.0 2.9 fusion.144
  151.1 5.0 fusion.146
  156.1 4.8 fusion.147
  160.9 7.3 %fusion.148 = f32[1024,3456]{1,0:T(8,128)} fusion(f32[1024,3456]{1,0:T(8,128)S(1)} %get-tuple-element.348, f32[1024]{0:T(1024)S(1)} %fusion.147, f32[1024]{0:T(1024)S(1)} %get-tuple-element.349, pred[128,3456]{1,0:T(8,128)(4,1)S(1)} %copy.27), kind=kLoop, calls=%fused_computation.16.clone.1 | loop fusion | flops 14155776 | bytes 28762112 | tf_op jit(solution)/shard_map/while/body/eval_jaxpr/div | solution.py:64
  168.8 7.6 %fusion.150 = f32[1024]{0:T(1024)S(1)} fusion(bf16[3456,128]{1,0:T(8,128)(2,1)S(1)} %squeeze.46, f32[1024,3456]{1,0:T(8,128)} %fusion.148, bf16[4,1024,128]{1,2,0:T(8,128)(2,1)S(1)} %copy-done.2, s32[]{:T(128)} %get-tuple-element.382), kind=kOutput, calls=%fused_computation.32.clone.1 | convolution fusion | flops 909900800 | bytes 15306756 | tf_op jit(solution)/shard_map/while/body/eval_jaxpr/dot_general | solution.py:66
  177.8 5.1 multiply_convert_fusion.4
  182.9 5.1 convolution_multiply_fusion.3
  188.0 1.6 stack.26
  189.6 8.3 %fusion.149 = f32[3456,128]{1,0:T(8,128)} fusion(f32[1024,3456]{1,0:T(8,128)} %fusion.148, bf16[4,1024,128]{1,2,0:T(8,128)(2,1)S(1)} %copy-done.2, s32[]{:T(128)} %get-tuple-element.382), kind=kOutput, calls=%fused_computation.22.clone.1 | convolution fusion | flops 909508608 | bytes 16187396 | tf_op jit(solution)/shard_map/while/body/eval_jaxpr/dot_general | solution.py:18
  197.9 2.9 stack.25
  200.8 12.6 %fusion.151 = f32[2,64,16384]{2,1,0:T(8,128)} fusion(f32[2,64,16384]{2,1,0:T(8,128)} %get-tuple-element.383, f32[1,27,16384]{2,1,0:T(8,128)} %stack.25, f32[1,27,16384]{2,1,0:T(8,128)} %stack.26, pred[]{:T(512)S(6)} %compare.15, s32[27]{0:T(128)S(1)} %fusion.143, pred[27]{0:T(512)(128)(4,1)S(1)} %get-tuple-element.346), kind=kOutput, calls=%fused_computation.9.clone.1 | convolution fusion | flops 684559744 | bytes 20316296 | tf_op jit(solution)/shard_map/while/body/eval_jaxpr/dn,sdx->snx/dot_general | solution.py:112
  213.4 2.8 fusion.152
  216.2 2.9 fusion.144
  223.3 5.0 fusion.146
  228.3 4.8 fusion.147
  233.1 7.3 %fusion.148 = f32[1024,3456]{1,0:T(8,128)} fusion(f32[1024,3456]{1,0:T(8,128)S(1)} %get-tuple-element.348, f32[1024]{0:T(1024)S(1)} %fusion.147, f32[1024]{0:T(1024)S(1)} %get-tuple-element.349, pred[128,3456]{1,0:T(8,128)(4,1)S(1)} %copy.27), kind=kLoop, calls=%fused_computation.16.clone.1 | loop fusion | flops 14155776 | bytes 28762112 | tf_op jit(solution)/shard_map/while/body/eval_jaxpr/div | solution.py:64
  241.0 7.6 %fusion.150 = f32[1024]{0:T(1024)S(1)} fusion(bf16[3456,128]{1,0:T(8,128)(2,1)S(1)} %squeeze.46, f32[1024,3456]{1,0:T(8,128)} %fusion.148, bf16[4,1024,128]{1,2,0:T(8,128)(2,1)S(1)} %copy-done.2, s32[]{:T(128)} %get-tuple-element.382), kind=kOutput, calls=%fused_computation.32.clone.1 | convolution fusion | flops 909900800 | bytes 15306756 | tf_op jit(solution)/shard_map/while/body/eval_jaxpr/dot_general | solution.py:66
  250.0 5.2 multiply_convert_fusion.4
  255.2 5.1 convolution_multiply_fusion.3
  260.2 1.6 stack.26
  261.9 8.3 %fusion.149 = f32[3456,128]{1,0:T(8,128)} fusion(f32[1024,3456]{1,0:T(8,128)} %fusion.148, bf16[4,1024,128]{1,2,0:T(8,128)(2,1)S(1)} %copy-done.2, s32[]{:T(128)} %get-tuple-element.382), kind=kOutput, calls=%fused_computation.22.clone.1 | convolution fusion | flops 909508608 | bytes 16187396 | tf_op jit(solution)/shard_map/while/body/eval_jaxpr/dot_general | solution.py:18
  270.1 2.9 stack.25
  273.1 12.6 %fusion.151 = f32[2,64,16384]{2,1,0:T(8,128)} fusion(f32[2,64,16384]{2,1,0:T(8,128)} %get-tuple-element.383, f32[1,27,16384]{2,1,0:T(8,128)} %stack.25, f32[1,27,16384]{2,1,0:T(8,128)} %stack.26, pred[]{:T(512)S(6)} %compare.15, s32[27]{0:T(128)S(1)} %fusion.143, pred[27]{0:T(512)(128)(4,1)S(1)} %get-tuple-element.346), kind=kOutput, calls=%fused_computation.9.clone.1 | convolution fusion | flops 684559744 | bytes 20316296 | tf_op jit(solution)/shard_map/while/body/eval_jaxpr/dn,sdx->snx/dot_general | solution.py:112
  285.6 2.8 fusion.152
  288.5 2.9 fusion.144
  295.6 5.0 fusion.146
  300.6 4.8 fusion.147
  305.3 7.3 %fusion.148 = f32[1024,3456]{1,0:T(8,128)} fusion(f32[1024,3456]{1,0:T(8,128)S(1)} %get-tuple-element.348, f32[1024]{0:T(1024)S(1)} %fusion.147, f32[1024]{0:T(1024)S(1)} %get-tuple-element.349, pred[128,3456]{1,0:T(8,128)(4,1)S(1)} %copy.27), kind=kLoop, calls=%fused_computation.16.clone.1 | loop fusion | flops 14155776 | bytes 28762112 | tf_op jit(solution)/shard_map/while/body/eval_jaxpr/div | solution.py:64
  313.2 7.6 %fusion.150 = f32[1024]{0:T(1024)S(1)} fusion(bf16[3456,128]{1,0:T(8,128)(2,1)S(1)} %squeeze.46, f32[1024,3456]{1,0:T(8,128)} %fusion.148, bf16[4,1024,128]{1,2,0:T(8,128)(2,1)S(1)} %copy-done.2, s32[]{:T(128)} %get-tuple-element.382), kind=kOutput, calls=%fused_computation.32.clone.1 | convolution fusion | flops 909900800 | bytes 15306756 | tf_op jit(solution)/shard_map/while/body/eval_jaxpr/dot_general | solution.py:66
  322.2 5.1 multiply_convert_fusion.4
  327.4 5.1 convolution_multiply_fusion.3
  332.5 1.6 stack.26
  334.1 8.3 %fusion.149 = f32[3456,128]{1,0:T(8,128)} fusion(f32[1024,3456]{1,0:T(8,128)} %fusion.148, bf16[4,1024,128]{1,2,0:T(8,128)(2,1)S(1)} %copy-done.2, s32[]{:T(128)} %get-tuple-element.382), kind=kOutput, calls=%fused_computation.22.clone.1 | convolution fusion | flops 909508608 | bytes 16187396 | tf_op jit(solution)/shard_map/while/body/eval_jaxpr/dot_general | solution.py:18
  342.4 2.9 stack.25
  345.3 12.6 %fusion.151 = f32[2,64,16384]{2,1,0:T(8,128)} fusion(f32[2,64,16384]{2,1,0:T(8,128)} %get-tuple-element.383, f32[1,27,16384]{2,1,0:T(8,128)} %stack.25, f32[1,27,16384]{2,1,0:T(8,128)} %stack.26, pred[]{:T(512)S(6)} %compare.15, s32[27]{0:T(128)S(1)} %fusion.143, pred[27]{0:T(512)(128)(4,1)S(1)} %get-tuple-element.346), kind=kOutput, calls=%fused_computation.9.clone.1 | convolution fusion | flops 684559744 | bytes 20316296 | tf_op jit(solution)/shard_map/while/body/eval_jaxpr/dn,sdx->snx/dot_general | solution.py:112
  357.9 2.8 fusion.152
  360.7 9.3 %reshape.344 = f32[2,8192,128]{2,1,0:T(8,128)} reshape(f32[2,64,16384]{2,1,0:T(8,128)} %get-tuple-element.125) | data formatting | bytes 16777216 | tf_op jit(solution)/shard_map/reshape | solution.py:123
  370.9 1.9 mul.193
  372.8 2.9 mul.194
  375.8 2.7 reshape.343
  378.4 2.5 multiply_reduce_fusion
  383.3 4.7 multiply_convert_fusion.1
  388.0 81.4 %reduce-scatter.2.cloned.1.call-done = f32[2,512,128]{2,1,0:T(8,128)} async-done(((f32[2,8192,128]{2,1,0:T(8,128)}), f32[2,512,128]{2,1,0:T(8,128)}) %reduce-scatter.2.cloned.1.call-update) | async-done | bytes 524304 | tf_op jit(solution)/shard_map/reduce_scatter | solution.py:171
  470.7 65.9 %all-reduce = (f32[128]{0:T(128)}, f32[128]{0:T(128)}) all-reduce(f32[128]{0:T(128)S(1)} %get-tuple-element.201, f32[128]{0:T(128)S(1)} %get-tuple-element.203), channel_id=1, replica_groups=mesh['dp'=8,'ctx'=16] {'dp','ctx'}, use_global_device_ids=true, to_apply=%region_16.17 | all-reduce | flops 256 | bytes 2048 | tf_op jit(solution)/shard_map/psum | solution.py:173
  536.6 1.6 slice.34
  538.2 1.8 fusion.72
  (297 shorter events, 81.0 us)
Async XLA Ops:
  7.2 46.9 %copy-start.11 = (bf16[1,512,1024]{2,1,0:T(8,128)(2,1)S(1)}, bf16[1,512,1024]{2,1,0:T(8,128)(2,1)}, u32[]{:S(2)}) copy-start(bf16[1,512,1024]{2,1,0:T(8,128)(2,1)} %param.16) | copy-start | bytes 3145732
  7.2 47.7 %copy-start.19 = (s32[1,4]{1,0:T(1,128)S(1)}, s32[1,4]{1,0:T(1,128)}, u32[]{:S(2)}) copy-start(s32[1,4]{1,0:T(1,128)} %param.21) | copy-start | bytes 52
  7.2 59.7 %all-gather.2.cloned.1.call-start = ((), (), s32[]{:S(2)}) async-start(), calls=%async_computation.1 | async-start | bytes 4456448 | tf_op jit(solution)/shard_map/all_gather | solution.py:158
  8.4 0.6 copy-start.14
  11.7 457.8 %reduce-scatter.2.cloned.1.call-start = ((), (), s32[]{:S(2)}) async-start(), calls=%async_computation.2 | async-start | bytes 8912896 | tf_op jit(solution)/shard_map/reduce_scatter | solution.py:171
  54.9 2.8 copy-start.5
  58.1 7.3 %copy-start.3 = (f32[4,1024,128]{2,1,0:T(8,128)}, f32[4,1024,128]{2,1,0:T(8,128)S(1)}, u32[]{:S(2)}) copy-start(f32[4,1024,128]{2,1,0:T(8,128)S(1)} %reshape.346) | copy-start | bytes 6291460
  58.4 6.0 %copy-start.7 = (bf16[4,1024,128]{1,2,0:T(8,128)(2,1)S(1)}, bf16[4,1024,128]{1,2,0:T(8,128)(2,1)}, u32[]{:S(2)}) copy-start(bf16[4,1024,128]{1,2,0:T(8,128)(2,1)} %copy.21) | copy-start | bytes 3145732
  58.4 7.0 %copy-start.17 = (f32[128]{0:T(128)S(1)}, f32[128]{0:T(128)}, u32[]{:S(2)}) copy-start(f32[128]{0:T(128)} %param.17) | copy-start | bytes 1540
  64.1 10.1 %copy-start.8 = (f32[512,8]{1,0:T(8,128)}, f32[512,8]{1,0:T(8,128)S(1)}, u32[]{:S(2)}) copy-start(f32[512,8]{1,0:T(8,128)S(1)} %add_rsqrt_fusion) | copy-start | bytes 49156
  64.3 9.9 %copy-start.12 = (f32[4,1024]{1,0:T(4,128)}, f32[4,1024]{1,0:T(4,128)S(1)}, u32[]{:S(2)}) copy-start(f32[4,1024]{1,0:T(4,128)S(1)} %rsqrt.21) | copy-start | bytes 49156
  91.1 7.9 %copy-start.2 = (bf16[4,1024,128]{1,2,0:T(8,128)(2,1)S(1)}, bf16[4,1024,128]{1,2,0:T(8,128)(2,1)}, u32[]{:S(2)}) copy-start(bf16[4,1024,128]{1,2,0:T(8,128)(2,1)} %get-tuple-element.402) | copy-start | bytes 3145732 | tf_op jit(solution)/shard_map/while
  98.9 9.1 %copy-start = (f32[1024,3456]{1,0:T(8,128)S(1)}, f32[1024,3456]{1,0:T(8,128)}, u32[]{:S(2)}) copy-start(f32[1024,3456]{1,0:T(8,128)} %fusion.148) | copy-start | bytes 42467332 | tf_op jit(solution)/shard_map/while
  128.1 13.1 %slice-start = ((s8[7077888]{0:T(1024)(128)(4,1)}), s8[2883584]{0:T(1024)(128)(4,1)S(1)}, s32[]{:S(2)}) async-start(s8[7077888]{0:T(1024)(128)(4,1)} %bitcast.173), calls=%async_computation.3 | async-start | bytes 5767168 | tf_op jit(solution)/shard_map/while
  131.0 10.2 %slice-start.1 = ((s8[7077888]{0:T(1024)(128)(4,1)}), s8[4194304]{0:T(1024)(128)(4,1)S(1)}, s32[]{:S(2)}) async-start(s8[7077888]{0:T(1024)(128)(4,1)} %bitcast.173), calls=%async_computation.4 | async-start | bytes 8388608 | tf_op jit(solution)/shard_map/while
  131.0 10.2 %copy-start.1 = (bf16[3456,128]{1,0:T(8,128)(2,1)S(1)}, bf16[3456,128]{1,0:T(8,128)(2,1)}, u32[]{:S(2)}) copy-start(bf16[3456,128]{1,0:T(8,128)(2,1)} %squeeze.45) | copy-start | bytes 2654212 | tf_op jit(solution)/shard_map/while
  160.9 7.9 %copy-start.2 = (bf16[4,1024,128]{1,2,0:T(8,128)(2,1)S(1)}, bf16[4,1024,128]{1,2,0:T(8,128)(2,1)}, u32[]{:S(2)}) copy-start(bf16[4,1024,128]{1,2,0:T(8,128)(2,1)} %get-tuple-element.402) | copy-start | bytes 3145732 | tf_op jit(solution)/shard_map/while
  168.7 9.1 %copy-start = (f32[1024,3456]{1,0:T(8,128)S(1)}, f32[1024,3456]{1,0:T(8,128)}, u32[]{:S(2)}) copy-start(f32[1024,3456]{1,0:T(8,128)} %fusion.148) | copy-start | bytes 42467332 | tf_op jit(solution)/shard_map/while
  197.9 15.5 %slice-start = ((s8[7077888]{0:T(1024)(128)(4,1)}), s8[2883584]{0:T(1024)(128)(4,1)S(1)}, s32[]{:S(2)}) async-start(s8[7077888]{0:T(1024)(128)(4,1)} %bitcast.173), calls=%async_computation.3 | async-start | bytes 5767168 | tf_op jit(solution)/shard_map/while
  200.8 12.6 %slice-start.1 = ((s8[7077888]{0:T(1024)(128)(4,1)}), s8[4194304]{0:T(1024)(128)(4,1)S(1)}, s32[]{:S(2)}) async-start(s8[7077888]{0:T(1024)(128)(4,1)} %bitcast.173), calls=%async_computation.4 | async-start | bytes 8388608 | tf_op jit(solution)/shard_map/while
  200.8 12.6 %copy-start.1 = (bf16[3456,128]{1,0:T(8,128)(2,1)S(1)}, bf16[3456,128]{1,0:T(8,128)(2,1)}, u32[]{:S(2)}) copy-start(bf16[3456,128]{1,0:T(8,128)(2,1)} %squeeze.45) | copy-start | bytes 2654212 | tf_op jit(solution)/shard_map/while
  233.1 7.9 %copy-start.2 = (bf16[4,1024,128]{1,2,0:T(8,128)(2,1)S(1)}, bf16[4,1024,128]{1,2,0:T(8,128)(2,1)}, u32[]{:S(2)}) copy-start(bf16[4,1024,128]{1,2,0:T(8,128)(2,1)} %get-tuple-element.402) | copy-start | bytes 3145732 | tf_op jit(solution)/shard_map/while
  241.0 9.1 %copy-start = (f32[1024,3456]{1,0:T(8,128)S(1)}, f32[1024,3456]{1,0:T(8,128)}, u32[]{:S(2)}) copy-start(f32[1024,3456]{1,0:T(8,128)} %fusion.148) | copy-start | bytes 42467332 | tf_op jit(solution)/shard_map/while
  270.1 15.5 %slice-start = ((s8[7077888]{0:T(1024)(128)(4,1)}), s8[2883584]{0:T(1024)(128)(4,1)S(1)}, s32[]{:S(2)}) async-start(s8[7077888]{0:T(1024)(128)(4,1)} %bitcast.173), calls=%async_computation.3 | async-start | bytes 5767168 | tf_op jit(solution)/shard_map/while
  273.1 12.6 %slice-start.1 = ((s8[7077888]{0:T(1024)(128)(4,1)}), s8[4194304]{0:T(1024)(128)(4,1)S(1)}, s32[]{:S(2)}) async-start(s8[7077888]{0:T(1024)(128)(4,1)} %bitcast.173), calls=%async_computation.4 | async-start | bytes 8388608 | tf_op jit(solution)/shard_map/while
  273.1 12.6 %copy-start.1 = (bf16[3456,128]{1,0:T(8,128)(2,1)S(1)}, bf16[3456,128]{1,0:T(8,128)(2,1)}, u32[]{:S(2)}) copy-start(bf16[3456,128]{1,0:T(8,128)(2,1)} %squeeze.45) | copy-start | bytes 2654212 | tf_op jit(solution)/shard_map/while
  305.3 7.9 %copy-start.2 = (bf16[4,1024,128]{1,2,0:T(8,128)(2,1)S(1)}, bf16[4,1024,128]{1,2,0:T(8,128)(2,1)}, u32[]{:S(2)}) copy-start(bf16[4,1024,128]{1,2,0:T(8,128)(2,1)} %get-tuple-element.402) | copy-start | bytes 3145732 | tf_op jit(solution)/shard_map/while
  313.2 9.1 %copy-start = (f32[1024,3456]{1,0:T(8,128)S(1)}, f32[1024,3456]{1,0:T(8,128)}, u32[]{:S(2)}) copy-start(f32[1024,3456]{1,0:T(8,128)} %fusion.148) | copy-start | bytes 42467332 | tf_op jit(solution)/shard_map/while
  342.4 15.5 %slice-start = ((s8[7077888]{0:T(1024)(128)(4,1)}), s8[2883584]{0:T(1024)(128)(4,1)S(1)}, s32[]{:S(2)}) async-start(s8[7077888]{0:T(1024)(128)(4,1)} %bitcast.173), calls=%async_computation.3 | async-start | bytes 5767168 | tf_op jit(solution)/shard_map/while
  345.3 12.6 %slice-start.1 = ((s8[7077888]{0:T(1024)(128)(4,1)}), s8[4194304]{0:T(1024)(128)(4,1)S(1)}, s32[]{:S(2)}) async-start(s8[7077888]{0:T(1024)(128)(4,1)} %bitcast.173), calls=%async_computation.4 | async-start | bytes 8388608 | tf_op jit(solution)/shard_map/while
  345.3 12.6 %copy-start.1 = (bf16[3456,128]{1,0:T(8,128)(2,1)S(1)}, bf16[3456,128]{1,0:T(8,128)(2,1)}, u32[]{:S(2)}) copy-start(bf16[3456,128]{1,0:T(8,128)(2,1)} %squeeze.45) | copy-start | bytes 2654212 | tf_op jit(solution)/shard_map/while
  370.0 0.9 copy-start.9
  370.9 4.8 copy-start.18
  372.8 5.6 %copy-start.4 = (f32[4,1024,128]{2,1,0:T(8,128)S(1)}, f32[4,1024,128]{2,1,0:T(8,128)}, u32[]{:S(2)}) copy-start(f32[4,1024,128]{2,1,0:T(8,128)} %copy-done.3) | copy-start | bytes 6291460
  372.8 5.6 %copy-start.13 = (f32[4,1024]{1,0:T(4,128)S(1)}, f32[4,1024]{1,0:T(4,128)}, u32[]{:S(2)}) copy-start(f32[4,1024]{1,0:T(4,128)} %copy-done.12) | copy-start | bytes 49156
  381.0 2.3 copy-start.6
  383.3 86.2 %copy-start.10 = (bf16[1,512,128]{2,1,0:T(8,128)(2,1)S(1)}, bf16[1,512,128]{2,1,0:T(8,128)(2,1)}, u32[]{:S(2)}) copy-start(bf16[1,512,128]{2,1,0:T(8,128)(2,1)} %param.14) | copy-start | bytes 393220
  383.3 86.2 %copy-start.15 = (f32[512]{0:T(512)S(1)}, f32[512]{0:T(512)}, u32[]{:S(2)}) copy-start(f32[512]{0:T(512)} %copy-done.14) | copy-start | bytes 6148
  383.3 86.2 %copy-start.16 = (f32[128]{0:T(128)S(1)}, f32[128]{0:T(128)}, u32[]{:S(2)}) copy-start(f32[128]{0:T(128)} %param.18) | copy-start | bytes 1540
Sparse Core Ops, SparseCore 0:
  11.8 41.0 all-gather.1
  370.1 99.3 reduce-scatter.1
where the time goes:
time: 548 us; the launch traced here: 547 us
  matrix products  197 us (36%)
  local copies, waits for them, and re-layouts  110 us (20%)
  waiting for transfers between devices  81.5 us (15%)
  other arithmetic  76.1 us (14%)
  blocking collectives  65.9 us (12%)
  between operations  14.3 us (3%)
    reduce_scatter x1, waiting for transfers between devices, body(): lax.psum_scatter(gradients, 'ctx', scatter_dimension=1, tiled=True)  81.4 us
    psum x1, blocking collectives, body(): q_total, k_total = lax.psum((q_part, k_part), ('dp', 'ctx'))  65.9 us
    dot_general x9, matrix products, contract_first(): lax.dot_general(left, right, (((0,), (0,)), ((), ())), preferred_element_...  54.5 us
    dot_general x4, matrix products, step(): jnp.einsum('dn,sdx->snx', picker.astype(jnp.float32), block_grads, precis...  47.9 us
    dot_general x8, matrix products, contract_last(): lax.dot_general(left, right, (((1,), (1,)), ((), ())), preferred_element_...  40.5 us
    gather x26, local copies, waits for them, and re-layouts, climb(): block_parent[jnp.maximum(current, 0)]  37.2 us
    dot_general x4, matrix products, attend(): attn_out = jnp.dot(chances_b, vals_win, preferred_element_type=jnp.float32)  30.5 us
    div x4, other arithmetic, attend(): chances = weights / jnp.sum(weights, axis=1, keepdims=True)  29.4 us
  transfers between devices with their start and end apart: 2, of which 1 were waited for; matrix products, arithmetic and copies ran while one was open for 13% of the time, Pallas kernels for 0%

commit v1 on v0

v1 whole, which is shorter than its diff:
```python
import functools, math
import jax, jax.numpy as jnp
from jax import lax
from jax.experimental import pallas as pl
from jax.experimental.pallas import tpu as pltpu
from jax.sharding import PartitionSpec as P

BLK = 128
HEADS = 8
PROMPT = 16
REACH = 10
SLOTS = 30
OWN = PROMPT + REACH
POS = 27
RT = 1024
CBP = 8
CBL = 10
HT = RT // BLK
CS = 256
TPB = HEADS // HT
LOW = -1e30
F32 = jnp.float32
BF = jnp.bfloat16
SCALE = 1.0 / math.sqrt(128.0)
LOG2E = 1.4426950408889634
SL2 = SCALE * LOG2E


def nt(a, b):
    return lax.dot_general(a, b, (((1,), (1,)), ((), ())), preferred_element_type=F32)


def nn(a, b):
    return jnp.dot(a, b, preferred_element_type=F32)


def attend_kernel(dev_ref, len_ref, from_ref, qg_ref, q_ref, do_ref, kv_ref,
           gq_ref, away_ref, mine_ref, qpart_ref,
           qn, qt, dn, dt, kt, w_s, dp_s, m_s, s_s, f_s, dq_s, dk_ref, dv_ref):
    d = dev_ref[0]
    first = d * 4
    dk_ref[...] = jnp.zeros_like(dk_ref)
    dv_ref[...] = jnp.zeros_like(dv_ref)
    m_s[...] = jnp.full_like(m_s, LOW)
    s_s[...] = jnp.zeros_like(s_s)
    qpart_ref[...] = jnp.zeros_like(qpart_ref)
    gain = qg_ref[...]

    def slot_t(s, _):
        kt[s] = kv_ref[pl.ds(pl.multiple_of(s * BLK, BLK), BLK), 0:BLK].T
        return 0

    lax.fori_loop(0, SLOTS, slot_t, 0)

    def facts(i):
        b = first + i
        start = jnp.int32(PROMPT)
        off = jnp.int32(0)
        live = jnp.int32(BLK)
        for r in range(8):
            n = len_ref[r]
            c = (n + BLK - 1) // BLK
            inside = (b >= start) & (b < start + c)
            off = jnp.where(inside, b - start, off)
            live = jnp.where(inside, jnp.minimum(n - (b - start) * BLK, BLK), live)
            start = start + c
        return b, off, live

    def prep(i, _):
        b, off, live = facts(i)
        src = jnp.int32(0)
        for j in range(4):
            src = jnp.where(from_ref[j] == b, j, src)
        rows = pl.ds(pl.multiple_of(i * BLK, BLK), BLK)
        srow = pl.ds(pl.multiple_of(src * BLK, BLK), BLK)
        alive = (lax.broadcasted_iota(jnp.int32, (BLK, BLK), 0) < live).astype(F32)
        for h in range(HEADS):
            cols = pl.ds(h * BLK, BLK)
            x = q_ref[rows, cols].astype(F32)
            r = lax.rsqrt(jnp.mean(x * x, axis=-1, keepdims=True) + 1e-6)
            y = (x * r * gain).astype(BF)
            z = (do_ref[srow, cols].astype(F32) * alive).astype(BF)
            t = i * TPB + h // HT
            e = pl.ds((h % HT) * BLK, BLK)
            qn[t, e, :] = y
            qt[t, :, e] = y.T
            dn[t, e, :] = z
            dt[t, :, e] = z.T
        return 0

    lax.fori_loop(0, 4, prep, 0)

    def per_block(i, _):
        b, off, live = facts(i)
        n_prompt = jnp.minimum(b, PROMPT)
        n_prev = jnp.clip(b - PROMPT, 0, REACH)
        pc = (n_prompt + CBP - 1) // CBP
        lc = (REACH - n_prev) // CBL
        keyi = lax.broadcasted_iota(jnp.int32, (BLK, RT), 0)
        toki = lax.rem(lax.broadcasted_iota(jnp.int32, (BLK, RT), 1), BLK)
        bias = jnp.where((keyi <= toki) & (keyi < live), 0.0, LOW)

        def seen(pos):
            return jnp.where(pos < PROMPT, pos < n_prompt, pos - PROMPT >= REACH - off)

        def per_tile(g, _):
            t = i * TPB + g

            def row0(pos):
                return pl.multiple_of(jnp.where(pos < PROMPT, pos, pos + i) * BLK, BLK)

            def first_pass(pos, nb, diag):
                r0 = row0(pos)
                kc = kv_ref[pl.ds(r0, nb * BLK), 0:BLK]
                for x in range(0, RT, CS):
                    cs = slice(x, x + CS)
                    s = nn(kc, qt[t, :, cs])
                    for u in range(nb):
                        su = s[u * BLK:(u + 1) * BLK]
                        if diag:
                            su = su + bias[:, cs]
                        su = su.reshape(BLK // 8, 8, CS)
                        m = jnp.max(su, axis=0) * SL2
                        w = jnp.exp2(su * SL2 - m[None])
                        s_s[pos + u, :, cs] = jnp.sum(w, axis=0)
                        if diag:
                            m_s[pos + u, :, cs] = m
                        else:
                            m_s[pos + u, :, cs] = jnp.where(seen(pos + u), m, LOW)
                        w_s[pos + u, :, cs] = w.reshape(BLK, CS)

            def over(body, init):
                init = lax.fori_loop(0, pc, lambda c, x: body(c * CBP, CBP, False, x), init)
                init = lax.fori_loop(lc, REACH // CBL, lambda c, x: body(PROMPT + c * CBL, CBL, False, x), init)
                return body(POS - 1, 1, True, init)

            def p1(pos, nb, diag, x):
                first_pass(pos, nb, diag)
                return x

            over(p1, 0)
            m = m_s[...]
            top = jnp.max(jnp.max(m, axis=0), axis=0, keepdims=True)
            f = jnp.exp2(m - top[None])
            tot = jnp.sum(jnp.sum(f * s_s[...], axis=0), axis=0, keepdims=True)
            f_s[...] = f * (1.0 / tot)[None]

            drows = dn[t]
            def p3(pos, nb, diag, acc):
                r0 = row0(pos)
                vc = kv_ref[pl.ds(r0, nb * BLK), BLK:2 * BLK]
                accs, ps = [], []
                for x in range(0, RT, CS):
                    cs = slice(x, x + CS)
                    dp = nn(vc, dt[t, :, cs])
                    a = acc[:, cs]
                    pu = []
                    for u in range(nb):
                        du = dp[u * BLK:(u + 1) * BLK]
                        ch = (w_s[pos + u, :, cs].reshape(BLK // 8, 8, CS) * f_s[pos + u, :, cs][None]).reshape(BLK, CS)
                        chb = ch.astype(BF)
                        w_s[pos + u, :, cs] = ch
                        dp_s[pos + u, :, cs] = du
                        a = a + jnp.sum((chb.astype(F32) * du).reshape(BLK // 8, 8, CS), axis=0)
                        pu.append(chb)
                    accs.append(a)
                    ps.append(jnp.concatenate(pu, axis=0))
                p = jnp.concatenate(ps, axis=1)
                rows = pl.ds(r0, nb * BLK)
                dv_ref[rows, :] += nn(p, drows)
                return jnp.concatenate(accs, axis=1)

            delta = over(p3, jnp.zeros((8, RT), F32))
            delta = jnp.sum(delta, axis=0, keepdims=True)
            qrows = qn[t]

            def p4(pos, nb, diag, dq):
                r0 = row0(pos)
                dss = []
                for u in range(nb):
                    ch = w_s[pos + u]
                    dss.append((ch * (dp_s[pos + u] - delta)).astype(BF))
                ds = jnp.concatenate(dss, axis=0) if nb > 1 else dss[0]
                rows = pl.ds(r0, nb * BLK)
                dk_ref[rows, :] += nn(ds, qrows)
                slot = r0 // BLK
                ktc = jnp.concatenate([kt[slot + u] for u in range(nb)], axis=1) if nb > 1 else kt[slot]
                dq_s[...] += nn(ktc, ds)
                return 0

            dq_s[...] = jnp.zeros_like(dq_s)
            over(p4, 0)
            dqt = dq_s[...]
            dq = dqt.T * SCALE
            rows = pl.ds(pl.multiple_of(i * BLK, BLK), BLK)
            part = jnp.zeros((8, BLK), F32)
            for u in range(HT):
                cols = pl.ds(pl.multiple_of((g * HT + u) * BLK, BLK), BLK)
                x = q_ref[rows, cols].astype(F32)
                r = lax.rsqrt(jnp.mean(x * x, axis=-1, keepdims=True) + 1e-6)
                unit = x * r
                dqu = dq[u * BLK:(u + 1) * BLK]
                both = dqu * unit
                part = part + jnp.sum(both.reshape(BLK // 8, 8, BLK), axis=0)
                mean = jnp.mean(both * gain, axis=-1, keepdims=True)
                gq_ref[rows, cols] = (r * (dqu * gain - unit * mean)).astype(BF)
            qpart_ref[...] += part
            return 0

        lax.fori_loop(0, TPB, per_tile, 0)
        return 0

    lax.fori_loop(0, 4, per_block, 0)

    def hand_over(s, _):
        rows = pl.ds(pl.multiple_of(s * BLK, BLK), BLK)
        away_ref[rows, 0:BLK] = dk_ref[rows, :].astype(BF)
        away_ref[rows, BLK:2 * BLK] = dv_ref[rows, :].astype(BF)
        return 0

    lax.fori_loop(0, OWN, hand_over, 0)
    mine_ref[:, 0:BLK] = dk_ref[OWN * BLK:, :]
    mine_ref[:, BLK:2 * BLK] = dv_ref[OWN * BLK:, :]


VM = pl.BlockSpec(memory_space=pltpu.VMEM)
SM = pl.BlockSpec(memory_space=pltpu.SMEM)


def attend(dev, lens, frm, qg, q, do, kv):
    rows = SLOTS * BLK
    return pl.pallas_call(
        attend_kernel,
        out_shape=(
            jax.ShapeDtypeStruct((512, 1024), BF),
            jax.ShapeDtypeStruct((OWN * BLK, 2 * BLK), BF),
            jax.ShapeDtypeStruct((4 * BLK, 2 * BLK), F32),
            jax.ShapeDtypeStruct((8, BLK), F32),
        ),
        in_specs=[SM, SM, SM, VM, VM, VM, VM],
        out_specs=(VM, VM, VM, VM),
        scratch_shapes=[
            pltpu.VMEM((4096 // RT, RT, BLK), BF),
            pltpu.VMEM((4096 // RT, BLK, RT), BF),
            pltpu.VMEM((4096 // RT, RT, BLK), BF),
            pltpu.VMEM((4096 // RT, BLK, RT), BF),
            pltpu.VMEM((SLOTS, BLK, BLK), BF),
            pltpu.VMEM((POS, BLK, RT), F32),
            pltpu.VMEM((POS, BLK, RT), F32),
            pltpu.VMEM((POS, 8, RT), F32),
            pltpu.VMEM((POS, 8, RT), F32),
            pltpu.VMEM((POS, 8, RT), F32),
            pltpu.VMEM((BLK, RT), F32),
            pltpu.VMEM((rows, BLK), F32),
            pltpu.VMEM((rows, BLK), F32),
        ],
        compiler_params=pltpu.CompilerParams(vmem_limit_bytes=60 * 1024 * 1024),
    )(dev, lens, frm, qg, q, do, kv)


MESH = pl.DeviceIdType.MESH
GRP = 512


def copy_to(src, dst, send, recv, dp, ctx):
    return pltpu.make_async_remote_copy(
        src_ref=src, dst_ref=dst, send_sem=send, recv_sem=recv,
        device_id=(dp, ctx), device_id_type=MESH)


def greet(dp, me, others):
    barrier = pltpu.get_barrier_semaphore()
    for ctx_off in range(1, 16):
        pl.semaphore_signal(barrier, inc=1, device_id=(dp, lax.rem(me + ctx_off, 16)), device_id_type=MESH)
    for dp_off in range(1, 8 if others else 1):
        pl.semaphore_signal(barrier, inc=1, device_id=(lax.rem(dp + dp_off, 8), me), device_id_type=MESH)
    pl.semaphore_wait(barrier, 22 if others else 15)


def spread_kernel(kg_ref, k_ref, v_ref, kv_ref, send_p, recv_p, send_l, recv_l):
    dp = lax.axis_index("dp")
    me = lax.axis_index("ctx")
    kv_ref[PROMPT * BLK:OWN * BLK, :] = jnp.zeros((REACH * BLK, 2 * BLK), BF)
    x = k_ref[...].astype(F32)
    r = lax.rsqrt(jnp.mean(x * x, axis=-1, keepdims=True) + 1e-6)
    mine = kv_ref.at[pl.ds(OWN * BLK, GRP)]
    kv_ref[OWN * BLK:, 0:BLK] = (x * r * kg_ref[...]).astype(BF)
    kv_ref[OWN * BLK:, BLK:2 * BLK] = v_ref[...]
    greet(dp, me, False)

    def slot(g):
        return kv_ref.at[pl.ds(pl.multiple_of(g * GRP, GRP), GRP)]

    def to_all(o):
        return copy_to(mine, slot(me), send_p.at[o], recv_p.at[me], dp, lax.rem(me + o, 16))

    locals_ = []
    for k in (1, 2, 3):
        n = 4 if k < 3 else 2
        src = kv_ref.at[pl.ds((OWN + 4 - n) * BLK, n * BLK)]
        dst = kv_ref.at[pl.ds((OWN + 4 - 4 * k - n) * BLK, n * BLK)]
        locals_.append(copy_to(src, dst, send_l.at[k - 1], recv_l.at[k - 1], dp, lax.rem(me + k, 16)))

    @pl.when(me < 4)
    def _():
        for o in range(15, 0, -1):
            to_all(o).start()
        kv_ref[pl.ds(pl.multiple_of(me * GRP, GRP), GRP), :] = kv_ref[OWN * BLK:, :]

    for k in (1, 2, 3):
        @pl.when((me >= 4) & (me + k < 16))
        def _(k=k):
            locals_[k - 1].start()
    for k in (1, 2, 3):
        @pl.when(me - k >= 4)
        def _(k=k):
            locals_[k - 1].wait_recv()
    for g in range(4):
        @pl.when(me != g)
        def _(g=g):
            copy_to(mine, slot(g), send_p.at[0], recv_p.at[g], dp, lax.rem(me + 1, 16)).wait_recv()
    for k in (1, 2, 3):
        @pl.when((me >= 4) & (me + k < 16))
        def _(k=k):
            locals_[k - 1].wait_send()

    @pl.when(me < 4)
    def _():
        for o in range(1, 16):
            to_all(o).wait_send()


def spread(kg, k, v):
    return pl.pallas_call(
        spread_kernel,
        out_shape=jax.ShapeDtypeStruct((SLOTS * BLK, 2 * BLK), BF),
        in_specs=[VM, VM, VM],
        out_specs=VM,
        scratch_shapes=[pltpu.SemaphoreType.DMA((16,)), pltpu.SemaphoreType.DMA((4,)),
                        pltpu.SemaphoreType.DMA((3,)), pltpu.SemaphoreType.DMA((3,))],
        compiler_params=pltpu.CompilerParams(collective_id=0, has_side_effects=True),
    )(kg, k, v)


def collect_kernel(kg_ref, k_ref, away_ref, mine_ref, qpart_ref, gk_ref, gv_ref, gain_ref,
                   bufa, bufb, bufc, bufl, sa, sb, tot, gown, gall, gdp,
                   send_a, recv_a, send_b, recv_b, send_c, recv_c, send_l, recv_l, send_g, recv_g):
    dp = lax.axis_index("dp")
    me = lax.axis_index("ctx")
    z = me // 4
    y = lax.rem(me // 2, 2)
    c = lax.rem(me, 2)
    greet(dp, me, True)
    sib = me + 1 - 2 * c
    yny = me + 2 - 4 * y

    def group(ref, g):
        return ref.at[pl.ds(pl.multiple_of(g * GRP, GRP), GRP)]

    ca = [copy_to(group(away_ref, 2 * j + 1 - c), bufa.at[j], send_a.at[j], recv_a.at[j], dp, sib) for j in range(2)]
    for x in ca:
        x.start()
    lo = []
    for k in (1, 2, 3):
        n = 4 if k < 3 else 2
        src = away_ref.at[pl.ds((OWN + 4 - 4 * k - n) * BLK, n * BLK)]
        lo.append(copy_to(src, bufl.at[k - 1, pl.ds(0, n * BLK)], send_l.at[k - 1], recv_l.at[k - 1], dp, lax.rem(me + 16 - k, 16)))
        @pl.when(me - k >= 4)
        def _(k=k):
            lo[k - 1].start()
    for x in ca:
        x.wait_recv()
    far = group(away_ref, 2 * (1 - y) + c)
    near = group(away_ref, 2 * y + c)
    sa[...] = (far[...].astype(F32) + bufa[1 - y].astype(F32)).astype(BF)
    cb = copy_to(sa, bufb, send_b, recv_b, dp, yny)
    cb.start()
    tot[...] = near[...].astype(F32) + bufa[y].astype(F32)
    cb.wait_recv()
    tot[...] += bufb[...].astype(F32)

    def zto(zz):
        return zz * 4 + 2 * y + c

    def half(h):
        return pl.ds(h * 256, 256)

    def leg(h, target):
        return copy_to(sb.at[half(h)], bufc.at[h], send_c.at[h], recv_c.at[h], dp, zto(target))

    for h, (src, mid, last) in ((0, (3, 2, 1)), (1, (1, 2, 3))):
        @pl.when(z == src)
        def _(h=h, src=src):
            sb[half(h), :] = tot[half(h), :].astype(BF)
            leg(h, 2).start()
    for h, (src, mid, last) in ((0, (3, 2, 1)), (1, (1, 2, 3))):
        for stage, nxt in ((mid, last), (last, 0)):
            @pl.when(z == stage)
            def _(h=h, nxt=nxt):
                leg(h, nxt).wait_recv()
                sb[half(h), :] = (tot[half(h), :] + bufc[h].astype(F32)).astype(BF)
                leg(h, nxt).start()

    @pl.when(z == 0)
    def _():
        for h in (0, 1):
            leg(h, 0).wait_recv()
            tot[half(h), :] += bufc[h].astype(F32)

    @pl.when(z != 0)
    def _():
        tot[...] = mine_ref[...]
        for h in (0, 1):
            leg(h, 0).wait_send()
    @pl.when(z == 0)
    def _():
        tot[...] += mine_ref[...]

    for k in (1, 2, 3):
        @pl.when((me >= 4) & (me + k < 16))
        def _(k=k):
            n = 4 if k < 3 else 2
            lo[k - 1].wait_recv()
            tot[(4 - n) * BLK:, :] += bufl[k - 1, 0:n * BLK].astype(F32)

    x = k_ref[...].astype(F32)
    r = lax.rsqrt(jnp.mean(x * x, axis=-1, keepdims=True) + 1e-6)
    unit = x * r
    dk = tot[:, 0:BLK] * SCALE
    both = dk * unit
    gown[...] = jnp.zeros_like(gown)
    gown[0:1, :] = jnp.sum(qpart_ref[...], axis=0, keepdims=True)
    gown[1:2, :] = jnp.sum(both, axis=0, keepdims=True)
    cg = [copy_to(gown, gall.at[me], send_g.at[o - 1], recv_g.at[me], dp, lax.rem(me + o, 16)) for o in range(1, 16)]
    for q in cg:
        q.start()
    gall[me] = gown[...]
    gain = kg_ref[...]
    mean = jnp.mean(both * gain, axis=-1, keepdims=True)
    gk_ref[...] = (r * (dk * gain - unit * mean)).astype(BF)
    gv_ref[...] = tot[:, BLK:2 * BLK].astype(BF)
    for o in range(1, 16):
        p = lax.rem(me + o, 16)
        copy_to(gown, gall.at[p], send_g.at[o - 1], recv_g.at[p], dp, p).wait_recv()
    total = gall[0]
    for o in range(1, 16):
        total = total + gall[o]
    for q in cg:
        q.wait_send()
    gown[...] = total
    ch = [copy_to(gown, gdp.at[dp], send_g.at[14 + o], recv_g.at[16 + dp], lax.rem(dp + o, 8), me) for o in range(1, 8)]
    for q in ch:
        q.start()
    gdp[dp] = total
    for o in range(1, 8):
        p = lax.rem(dp + o, 8)
        copy_to(gown, gdp.at[p], send_g.at[14 + o], recv_g.at[16 + p], p, me).wait_recv()
    total = gdp[0]
    for o in range(1, 8):
        total = total + gdp[o]
    gain_ref[...] = total
    for q in ch:
        q.wait_send()
    for q in ca:
        q.wait_send()
    cb.wait_send()
    for k in (1, 2, 3):
        @pl.when(me - k >= 4)
        def _(k=k):
            lo[k - 1].wait_send()


def collect(kg, k, away, mine, qpart):
    dma = pltpu.SemaphoreType.DMA
    return pl.pallas_call(
        collect_kernel,
        out_shape=(
            jax.ShapeDtypeStruct((GRP, BLK), BF),
            jax.ShapeDtypeStruct((GRP, BLK), BF),
            jax.ShapeDtypeStruct((8, BLK), F32),
        ),
        in_specs=[VM] * 5,
        out_specs=(VM, VM, VM),
        scratch_shapes=[
            pltpu.VMEM((2, GRP, 2 * BLK), BF),
            pltpu.VMEM((GRP, 2 * BLK), BF),
            pltpu.VMEM((2, 256, 2 * BLK), BF),
            pltpu.VMEM((3, GRP, 2 * BLK), BF),
            pltpu.VMEM((GRP, 2 * BLK), BF),
            pltpu.VMEM((GRP, 2 * BLK), BF),
            pltpu.VMEM((GRP, 2 * BLK), F32),
            pltpu.VMEM((8, BLK), F32),
            pltpu.VMEM((16, 8, BLK), F32),
            pltpu.VMEM((8, 8, BLK), F32),
            dma((2,)), dma((2,)), dma, dma, dma((2,)), dma((2,)),
            dma((3,)), dma((3,)), dma((22,)), dma((24,)),
        ],
        compiler_params=pltpu.CompilerParams(collective_id=1, has_side_effects=True, vmem_limit_bytes=32 * 1024 * 1024),
    )(kg, k, away, mine, qpart)


def body(q_raw, k_raw, values, d_out, q_gain, k_gain, resp_len, block_parent, block_from):
    dev = lax.axis_index("ctx").astype(jnp.int32).reshape(1)
    kg = k_gain.reshape(1, BLK)
    kv = spread(kg, k_raw[0], values[0])
    gq, away, mine, qpart = attend(dev, resp_len[0], block_from[0], q_gain.reshape(1, BLK), q_raw[0], d_out[0], kv)
    gk, gv, gains = collect(kg, k_raw[0], away, mine, qpart)
    return gq[None], gk[None], gv[None], gains[0], gains[1]


def solution(mesh):
    tok = P("dp", "ctx", None)
    return jax.shard_map(
        body,
        mesh=mesh,
        in_specs=(tok, tok, tok, tok, P(), P(), P("dp", None), P("dp", None), P("dp", "ctx")),
        out_specs=(tok, tok, tok, P(), P()),
        check_vma=False,
    )
```

time: 548 us -> 171 us (0.31)
  matrix products: 197 us -> 0 us
  Pallas kernels: 0 us -> 165 us
  local copies, waits for them, and re-layouts: 110 us -> 5.02 us
  waiting for transfers between devices: 81.5 us -> 0 us
  other arithmetic: 76.1 us -> 0 us
  blocking collectives: 65.9 us -> 0 us
  between operations: 14.3 us -> 0.68 us
    dot_general x37 -> x0, matrix products: 197 us -> none  [the longest x9 54.5 us: contract_first(): lax.dot_general(left, right, (((0,), (0,)), ((), ())), preferred_element_...]
    pallas_call x0 -> x3, Pallas kernels: none -> 165 us  [the longest x1 72 us: collect(): pl.pallas_call(collect_kernel, out_shape=(jax.ShapeDtypeStruct((GRP, BLK)...]
    reduce_scatter x1 -> x0, waiting for transfers between devices: 81.4 us -> none  [body(): lax.psum_scatter(gradients, 'ctx', scatter_dimension=1, tiled=True)]
    psum x1 -> x0, blocking collectives: 65.9 us -> none  [body(): q_total, k_total = lax.psum((q_part, k_part), ('dp', 'ctx'))]
    gather x26 -> x0, local copies, waits for them, and re-layouts: 37.2 us -> none  [climb(): block_parent[jnp.maximum(current, 0)]]
    div x6 -> x0, other arithmetic: 29.4 us -> none  [the longest x4 29.4 us: attend(): chances = weights / jnp.sum(weights, axis=1, keepdims=True)]
    reduce_sum x9 -> x0, other arithmetic: 27.5 us -> none  [the longest x4 19 us: attend(): chances = weights / jnp.sum(weights, axis=1, keepdims=True)]
    reshape x4 -> x0, local copies, waits for them, and re-layouts: 20.6 us -> none  [the longest x1 9.28 us: block_pass(): return (gradients.reshape(2, store_blocks * BLK, head_size), query_grad)]
  transfers between devices with their start and end apart: 2 -> 0, of which waited for: 1 -> 0; matrix products, arithmetic and copies ran while one was open for 13% -> 0% of each run, Pallas kernels for 0% -> 0%
where the time goes in v1:
time: 171 us
  Pallas kernels  165 us (96%)
  local copies, waits for them, and re-layouts  5.02 us (3%)
    pallas_call x1, Pallas kernels, collect(): pl.pallas_call(collect_kernel, out_shape=(jax.ShapeDtypeStruct((GRP, BLK)...  72 us
    pallas_call x1, Pallas kernels, spread(): pl.pallas_call(spread_kernel, out_shape=jax.ShapeDtypeStruct((SLOTS * BLK...  63.3 us
    pallas_call x1, Pallas kernels, attend(): pl.pallas_call(attend_kernel, out_shape=(jax.ShapeDtypeStruct((512, 1024)...  30 us
    unnamed x12, local copies, waits for them, and re-layouts  4.5 us

profile of v1, /device:TPU:1, one launch (start us, length us, event | category | flops | bytes accessed | tf_op | source)
XLA Modules:
  0.0 171.0 jit_solution(14197384472907171143)
XLA Ops:
  0.6 63.3 %shard_map.119.kv_ref = bf16[3840,256]{1,0:T(8,128)(2,1)} custom-call(f32[1,128]{1,0:T(1,128)} %bitcast.20, bf16[512,128]{1,0:T(8,128)(2,1)} %bitcast.16, bf16[512,128]{1,0:T(8,128)(2,1)} %bitcast.24), custom_call_target="tpu_custom_call" | custom-call | tf_op jit(solution)/shard_map/pallas_call | solution.py:334
  64.0 0.0 copy-start.2
  64.0 0.0 copy-start.4
  64.0 30.0 %shard_map.120 = (bf16[512,1024]{1,0:T(8,128)(2,1)}, bf16[3328,256]{1,0:T(8,128)(2,1)}, f32[512,256]{1,0:T(8,128)}, f32[8,128]{1,0:T(8,128)}) custom-call(s32[1]{0:T(128)} %bitcast.dev_ref, s32[8]{0:T(128)} %bitcast.25, s32[4]{0:T(128)} %bitcast.26, f32[1,128]{1,0:T(1,128)} %bitcast.27, bf16[512,1024]{1,0:T(8,128)(2,1)} %bitcast.22, ...), custom_call_target="tpu_custom_call" | custom-call | tf_op jit(solution)/shard_map/pallas_call | solution.py:232
  93.9 0.0 copy-done.2
  93.9 0.0 copy-done.4
  93.9 0.0 copy-start
  94.0 1.4 copy-done
  95.4 0.0 copy-start.1
  95.4 1.0 copy-done.1
  96.4 0.0 copy-start.3
  96.4 0.7 copy-done.3
  97.1 72.0 %shard_map.121 = (bf16[512,128]{1,0:T(8,128)(2,1)S(1)}, bf16[512,128]{1,0:T(8,128)(2,1)S(1)}, f32[8,128]{1,0:T(8,128)S(1)}) custom-call(f32[1,128]{1,0:T(1,128)S(1)} %bitcast.21, bf16[512,128]{1,0:T(8,128)(2,1)S(1)} %bitcast.17, bf16[3328,256]{1,0:T(8,128)(2,1)S(1)} %copy-done, f32[512,256]{1,0:T(8,128)S(1)} %copy-done.1, f32[8,128]{1,0:T(8,128)S(1)} %copy-done.3), custom_call_target="tpu_custom_call" | custom-call | tf_op jit(solution)/shard_map/pallas_call | solution.py:475
  169.2 0.5 slice_bitcast_fusion
  169.7 0.7 copy.15
  170.3 0.7 copy.16
Async XLA Ops:
  64.0 30.0 %copy-start.2 = (bf16[1,512,128]{2,1,0:T(8,128)(2,1)S(1)}, bf16[1,512,128]{2,1,0:T(8,128)(2,1)}, u32[]{:S(2)}) copy-start(bf16[1,512,128]{2,1,0:T(8,128)(2,1)} %param.10) | copy-start | bytes 393220
  64.0 30.0 %copy-start.4 = (f32[128]{0:T(128)S(1)}, f32[128]{0:T(128)}, u32[]{:S(2)}) copy-start(f32[128]{0:T(128)} %param.14) | copy-start | bytes 1540
  93.9 1.5 copy-start
  95.4 1.0 copy-start.1
  96.4 0.7 copy-start.3

commit v2 on v1

v2 whole, which is shorter than its diff:
```python
import functools, math
import jax, jax.numpy as jnp
from jax import lax
from jax.experimental import pallas as pl
from jax.experimental.pallas import tpu as pltpu
from jax.sharding import PartitionSpec as P

BLK = 128
HEADS = 8
PROMPT = 16
REACH = 10
SLOTS = 30
OWN = PROMPT + REACH
POS = 27
RT = 1024
CBP = 8
CBL = 10
HT = RT // BLK
CS = 256
TPB = HEADS // HT
LOW = -1e30
F32 = jnp.float32
BF = jnp.bfloat16
SCALE = 1.0 / math.sqrt(128.0)
LOG2E = 1.4426950408889634
SL2 = SCALE * LOG2E
VM = pl.BlockSpec(memory_space=pltpu.VMEM)
SM = pl.BlockSpec(memory_space=pltpu.SMEM)


def nt(a, b):
    return lax.dot_general(a, b, (((1,), (1,)), ((), ())), preferred_element_type=F32)


def nn(a, b):
    return jnp.dot(a, b, preferred_element_type=F32)


MESH = pl.DeviceIdType.MESH
GRP = 512


def copy_to(src, dst, send, recv, dp, ctx):
    return pltpu.make_async_remote_copy(
        src_ref=src, dst_ref=dst, send_sem=send, recv_sem=recv,
        device_id=(dp, ctx), device_id_type=MESH)


def greet(dp, me, wide):
    barrier = pltpu.get_barrier_semaphore()
    c = lax.rem(me, 2)
    y = lax.rem(me // 2, 2)
    if wide:
        targets = [(dp, lax.rem(me + o, 16)) for o in range(1, 16)]
        targets += [(lax.rem(dp + o, 8), me) for o in range(1, 8)]
    else:
        targets = [(dp, me + 1 - 2 * c), (dp, me + 2 - 4 * y)]
        targets += [(dp, lax.rem(me + o, 16)) for o in (4, 12, 2, 14, 3, 13)]
    for t in targets:
        pl.semaphore_signal(barrier, inc=1, device_id=t, device_id_type=MESH)
    pl.semaphore_wait(barrier, len(targets))


def fused_kernel(len_ref, from_ref, qg_ref, kg_ref, q_ref, do_ref, k_ref, v_ref,
                 gq_ref, gk_ref, gv_ref, gain_ref,
                 kv_ref, qn, qt, dn, dt, kt, w_s, dp_s, m_s, s_s, f_s, dq_s, dk_ref, dv_ref, qpart,
                 away, bufa, bufb, bufc, bufl, bufs, sa, sb, sl, tot, gown, gall, gdp,
                 send_z, recv_z, send_y, recv_y, send_s, recv_s, fsend_l, frecv_l,
                 send_a, recv_a, send_b, recv_b, send_c, recv_c, send_l, recv_l, send_g, recv_g):
    dp = lax.axis_index("dp")
    me = lax.axis_index("ctx")
    z = me // 4
    y = lax.rem(me // 2, 2)
    c = lax.rem(me, 2)
    n = me // 2
    first = me * 4
    sib = me + 1 - 2 * c
    yny = me + 2 - 4 * y
    kv_ref[PROMPT * BLK:OWN * BLK, :] = jnp.zeros((REACH * BLK, 2 * BLK), BF)
    x = k_ref[...].astype(F32)
    r = lax.rsqrt(jnp.mean(x * x, axis=-1, keepdims=True) + 1e-6)
    kv_ref[OWN * BLK:, 0:BLK] = (x * r * kg_ref[...]).astype(BF)
    kv_ref[OWN * BLK:, BLK:2 * BLK] = v_ref[...]

    @pl.when(z == 0)
    def _():
        kv_ref[pl.ds(pl.multiple_of(me * GRP, GRP), GRP), :] = kv_ref[OWN * BLK:, :]

    greet(dp, me, True)
    chain = 2 * y + c
    other = 2 * (1 - y) + c

    def krows(g, h):
        return kv_ref.at[pl.ds(pl.multiple_of(g * GRP + h * 256, 256), 256)]

    def kblocks(first, count):
        return kv_ref.at[pl.ds(first * BLK, count * BLK)]

    def kv_z(h, zz, k):
        return copy_to(krows(chain, h), krows(chain, h), send_z.at[k], recv_z.at[h], dp, zz * 4 + chain)

    def kv_y(h):
        return copy_to(krows(chain, h), krows(chain, h), send_y.at[h], recv_y.at[h], dp, yny)

    def kv_s(j, h):
        g = chain if j == 0 else other
        return copy_to(krows(g, h), krows(g, h), send_s.at[2 * j + h], recv_s.at[2 * j + h], dp, sib)

    has_next = (n >= 2) & (n + 1 <= 7)
    has_prev = n >= 3
    ahead = copy_to(kblocks(OWN, 4),kblocks(PROMPT + 2, 4), fsend_l.at[0], frecv_l.at[0], dp, lax.rem(me + 2, 16))
    own_sib = copy_to(kblocks(OWN, 4),kblocks(PROMPT + 6, 4), fsend_l.at[1], frecv_l.at[1], dp, sib)
    kfar = copy_to(kblocks(OWN + 2, 2),kblocks(PROMPT, 2), fsend_l.at[2], frecv_l.at[2], dp, lax.rem(me + 3, 16))
    relay_full = copy_to(kblocks(PROMPT + 2, 4),kblocks(PROMPT + 6, 4), fsend_l.at[3], frecv_l.at[1], dp, sib)
    relay_half = copy_to(kblocks(PROMPT + 4, 2),kblocks(PROMPT, 2), fsend_l.at[4], frecv_l.at[2], dp, sib)
    sends_kfar = (c == 1) & (n >= 2) & (n + 2 <= 7)
    gets_kfar = (c == 0) & (n >= 4)

    @pl.when(z == 0)
    def _():
        kv_z(0, 1, 0).start()
        kv_z(1, 3, 1).start()
        kv_z(1, 1, 2).start()
        kv_z(0, 3, 3).start()
        for h in (0, 1):
            kv_y(h).start()
            kv_s(0, h).start()

    @pl.when((c == 0) & (n >= 2))
    def _():
        own_sib.start()

    @pl.when(has_next)
    def _():
        ahead.start()

    @pl.when(sends_kfar)
    def _():
        kfar.start()

    early = jnp.where(z == 1, 1, 0)
    order = (early, 1 - early)

    def half(h):
        return pl.ds(pl.multiple_of(h * 256, 256), 256)

    def rows(g, h):
        return pl.ds(pl.multiple_of(g * GRP + h * 256, 256), 256)

    def blocks(first, count):
        return pl.ds(first * BLK, count * BLK)

    def cp_a(j, h):
        return copy_to(away.at[rows(2 * j + 1 - c, h)], bufa.at[j, half(h)],
                       send_a.at[2 * j + h], recv_a.at[2 * j + h], dp, sib)

    def cp_b(h):
        return copy_to(sa.at[half(h)], bufb.at[half(h)], send_b.at[h], recv_b.at[h], dp, yny)

    def cp_c(h, slot, zz):
        return copy_to(sb.at[half(h)], bufc.at[slot, half(h)], send_c.at[h], recv_c.at[2 * slot + h],
                       dp, zz * 4 + 2 * y + c)

    has_prev = n >= 3
    from_next = (n >= 2) & (n + 1 <= 7)
    hand_full = copy_to(away.at[blocks(PROMPT + 6, 4)], bufs, send_l.at[0], recv_l.at[0], dp, sib)
    hand_half = copy_to(away.at[blocks(PROMPT, 2)], bufs.at[pl.ds(0, 2 * BLK)], send_l.at[1], recv_l.at[0], dp, sib)
    back = copy_to(sl, bufl.at[0], send_l.at[2], recv_l.at[1], dp, lax.rem(me + 14, 16))
    near_back = copy_to(away.at[blocks(PROMPT + 6, 4)], bufl.at[1], send_l.at[3], recv_l.at[2], dp, sib)
    far_back = copy_to(away.at[blocks(PROMPT, 2)], bufl.at[2, pl.ds(0, 2 * BLK)], send_l.at[4], recv_l.at[3],
                       dp, lax.rem(me + 13, 16))
    sends_near = (c == 1) & (n >= 2)
    gets_near = (c == 0) & (n >= 2)
    sends_far = (c == 0) & (n >= 4)
    gets_far = (c == 1) & (n >= 2) & (n + 2 <= 7)

    def hand_over(s, _):
        rr = pl.ds(pl.multiple_of(s * BLK, BLK), BLK)
        away[rr, 0:BLK] = dk_ref[rr, :].astype(BF)
        away[rr, BLK:2 * BLK] = dv_ref[rr, :].astype(BF)
        return 0

    def local_sends():
        @pl.when(has_prev & (c == 0))
        def _():
            hand_full.start()

        @pl.when(has_prev & (c == 1))
        def _():
            hand_half.start()

        @pl.when(sends_near)
        def _():
            near_back.start()

        @pl.when(sends_far)
        def _():
            far_back.start()

    dk_ref[...] = jnp.zeros_like(dk_ref)
    dv_ref[...] = jnp.zeros_like(dv_ref)
    m_s[...] = jnp.full_like(m_s, LOW)
    s_s[...] = jnp.zeros_like(s_s)
    qpart[...] = jnp.zeros_like(qpart)
    gain = qg_ref[...]

    def facts(i):
        b = first + i
        start = jnp.int32(PROMPT)
        off = jnp.int32(0)
        live = jnp.int32(BLK)
        for r in range(8):
            n = len_ref[r]
            c = (n + BLK - 1) // BLK
            inside = (b >= start) & (b < start + c)
            off = jnp.where(inside, b - start, off)
            live = jnp.where(inside, jnp.minimum(n - (b - start) * BLK, BLK), live)
            start = start + c
        return b, off, live

    def prep(i, _):
        b, off, live = facts(i)
        src = jnp.int32(0)
        for j in range(4):
            src = jnp.where(from_ref[j] == b, j, src)
        rows = pl.ds(pl.multiple_of(i * BLK, BLK), BLK)
        srcv = jnp.full((BLK, BLK), src, jnp.int32)
        alive = (lax.broadcasted_iota(jnp.int32, (BLK, BLK), 0) < live).astype(F32)
        for h in range(HEADS):
            cols = pl.ds(h * BLK, BLK)
            x = q_ref[rows, cols].astype(F32)
            r = lax.rsqrt(jnp.mean(x * x, axis=-1, keepdims=True) + 1e-6)
            y = (x * r * gain).astype(BF)
            z = do_ref[0:BLK, cols].astype(F32)
            for j in range(1, 4):
                z = jnp.where(srcv == j, do_ref[j * BLK:(j + 1) * BLK, cols].astype(F32), z)
            z = (z * alive).astype(BF)
            t = i * TPB + h // HT
            e = pl.ds((h % HT) * BLK, BLK)
            qn[t, e, :] = y
            qt[t, :, e] = y.T
            dn[t, e, :] = z
            dt[t, :, e] = z.T
        return 0

    lax.fori_loop(0, 2, prep, 0)
    def got(h):
        kv_z(h, 0, 0).wait_recv()
        kv_y(h).start()
        kv_s(0, h).start()

    @pl.when(z == 1)
    def _():
        kv_z(0, 2, 0).wait_recv()
        kv_z(0, 2, 0).start()
        kv_y(0).start()
        kv_s(0, 0).start()
        got(1)

    @pl.when(z == 3)
    def _():
        kv_z(1, 2, 0).wait_recv()
        kv_z(1, 2, 0).start()
        kv_y(1).start()
        kv_s(0, 1).start()
        got(0)

    @pl.when(z == 2)
    def _():
        got(0)
        got(1)

    lax.fori_loop(2, 4, prep, 0)
    @pl.when(has_prev)
    def _():
        ahead.wait_recv()

    @pl.when(has_prev & (c == 1))
    def _():
        relay_full.start()

    @pl.when(has_prev & (c == 0))
    def _():
        relay_half.start()

    def y_got(h):
        copy_to(krows(other, h), krows(other, h), send_y.at[h], recv_y.at[h], dp, yny).wait_recv()
        kv_s(1, h).start()

    @pl.when(z != 3)
    def _():
        y_got(0)
        y_got(1)

    @pl.when(z == 3)
    def _():
        y_got(1)
        y_got(0)

    for j in (0, 1):
        for h in (0, 1):
            g = (2 * y + 1 - c) if j == 0 else (2 * (1 - y) + 1 - c)
            copy_to(krows(g, h), krows(g, h), send_s.at[2 * j + h], recv_s.at[2 * j + h], dp, sib).wait_recv()

    @pl.when(((c == 1) & (n >= 2)) | ((c == 0) & has_prev))
    def _():
        own_sib.wait_recv()

    @pl.when(gets_kfar | ((c == 1) & has_prev))
    def _():
        kfar.wait_recv()

    def slot_t(s, _):
        kt[s] = kv_ref[pl.ds(pl.multiple_of(s * BLK, BLK), BLK), 0:BLK].T
        return 0

    lax.fori_loop(0, SLOTS, slot_t, 0)

    def per_block(i, _):
        b, off, live = facts(i)
        n_prompt = jnp.minimum(b, PROMPT)
        n_prev = jnp.clip(b - PROMPT, 0, REACH)
        pc = (n_prompt + CBP - 1) // CBP
        lc = (REACH - n_prev) // CBL
        keyi = lax.broadcasted_iota(jnp.int32, (BLK, RT), 0)
        toki = lax.rem(lax.broadcasted_iota(jnp.int32, (BLK, RT), 1), BLK)
        bias = jnp.where((keyi <= toki) & (keyi < live), 0.0, LOW)

        offv = jnp.full((8, CS), off, jnp.int32)

        def seen(pos):
            prompt = pos < PROMPT
            spare = jnp.where(prompt, n_prompt - 1 - pos, pos - PROMPT - REACH)
            return spare + offv * jnp.where(prompt, 0, 1) >= 0

        def per_tile(g, _):
            t = i * TPB + g

            def row0(pos):
                return pl.multiple_of(jnp.where(pos < PROMPT, pos, pos + i) * BLK, BLK)

            def first_pass(pos, nb, diag):
                r0 = row0(pos)
                kc = kv_ref[pl.ds(r0, nb * BLK), 0:BLK]
                for x in range(0, RT, CS):
                    cs = slice(x, x + CS)
                    s = nn(kc, qt[t, :, cs])
                    for u in range(nb):
                        su = s[u * BLK:(u + 1) * BLK]
                        if diag:
                            su = su + bias[:, cs]
                        su = su.reshape(BLK // 8, 8, CS)
                        m = jnp.max(su, axis=0) * SL2
                        w = jnp.exp2(su * SL2 - m[None])
                        s_s[pos + u, :, cs] = jnp.sum(w, axis=0)
                        if diag:
                            m_s[pos + u, :, cs] = m
                        else:
                            m_s[pos + u, :, cs] = jnp.where(seen(pos + u), m, LOW)
                        w_s[pos + u, :, cs] = w.reshape(BLK, CS)

            def over(body, init):
                init = lax.fori_loop(0, pc, lambda c, x: body(c * CBP, CBP, False, x), init)
                init = lax.fori_loop(lc, REACH // CBL, lambda c, x: body(PROMPT + c * CBL, CBL, False, x), init)
                return body(POS - 1, 1, True, init)

            def p1(pos, nb, diag, x):
                first_pass(pos, nb, diag)
                return x

            over(p1, 0)
            m = m_s[...]
            top = jnp.max(jnp.max(m, axis=0), axis=0, keepdims=True)
            f = jnp.exp2(m - top[None])
            tot = jnp.sum(jnp.sum(f * s_s[...], axis=0), axis=0, keepdims=True)
            f_s[...] = f * (1.0 / tot)[None]

            drows = dn[t]
            def p3(pos, nb, diag, acc):
                r0 = row0(pos)
                vc = kv_ref[pl.ds(r0, nb * BLK), BLK:2 * BLK]
                accs, ps = [], []
                for x in range(0, RT, CS):
                    cs = slice(x, x + CS)
                    dp = nn(vc, dt[t, :, cs])
                    a = acc[:, cs]
                    pu = []
                    for u in range(nb):
                        du = dp[u * BLK:(u + 1) * BLK]
                        ch = (w_s[pos + u, :, cs].reshape(BLK // 8, 8, CS) * f_s[pos + u, :, cs][None]).reshape(BLK, CS)
                        chb = ch.astype(BF)
                        w_s[pos + u, :, cs] = ch
                        dp_s[pos + u, :, cs] = du
                        a = a + jnp.sum((chb.astype(F32) * du).reshape(BLK // 8, 8, CS), axis=0)
                        pu.append(chb)
                    accs.append(a)
                    ps.append(jnp.concatenate(pu, axis=0))
                p = jnp.concatenate(ps, axis=1)
                rows = pl.ds(r0, nb * BLK)
                dv_ref[rows, :] += nn(p, drows)
                return jnp.concatenate(accs, axis=1)

            delta = over(p3, jnp.zeros((8, RT), F32))
            delta = jnp.sum(delta, axis=0, keepdims=True)
            qrows = qn[t]

            def p4(pos, nb, diag, dq):
                r0 = row0(pos)
                dss = []
                for u in range(nb):
                    ch = w_s[pos + u]
                    dss.append((ch * (dp_s[pos + u] - delta)).astype(BF))
                ds = jnp.concatenate(dss, axis=0) if nb > 1 else dss[0]
                rows = pl.ds(r0, nb * BLK)
                dk_ref[rows, :] += nn(ds, qrows)
                slot = r0 // BLK
                ktc = jnp.concatenate([kt[slot + u] for u in range(nb)], axis=1) if nb > 1 else kt[slot]
                dq_s[...] += nn(ktc, ds)
                return 0

            dq_s[...] = jnp.zeros_like(dq_s)
            p4(POS - 1, 1, True, 0)
            lax.fori_loop(lc, REACH // CBL, lambda c, x: p4(PROMPT + c * CBL, CBL, False, x), 0)

            @pl.when(i == 3)
            def _():
                lax.fori_loop(PROMPT, OWN, hand_over, 0)
                local_sends()

            def p4_prompt(j, _):
                @pl.when(j < pc)
                def _():
                    p4(j * CBP, CBP, False, 0)

                @pl.when(i == 3)
                def _():
                    lax.fori_loop(8 * j, 8 * j + 8, hand_over, 0)
                    for h in order:
                        cp_a(j, h).start()

                return 0

            lax.fori_loop(0, 2, p4_prompt, 0)
            dqt = dq_s[...]
            dq = dqt.T * SCALE
            rows = pl.ds(pl.multiple_of(i * BLK, BLK), BLK)
            part = jnp.zeros((8, BLK), F32)
            for u in range(HT):
                cols = pl.ds(pl.multiple_of((g * HT + u) * BLK, BLK), BLK)
                x = q_ref[rows, cols].astype(F32)
                r = lax.rsqrt(jnp.mean(x * x, axis=-1, keepdims=True) + 1e-6)
                unit = x * r
                dqu = dq[u * BLK:(u + 1) * BLK]
                both = dqu * unit
                part = part + jnp.sum(both.reshape(BLK // 8, 8, BLK), axis=0)
                mean = jnp.mean(both * gain, axis=-1, keepdims=True)
                gq_ref[rows, cols] = (r * (dqu * gain - unit * mean)).astype(BF)
            qpart[...] += part
            return 0

        lax.fori_loop(0, TPB, per_tile, 0)
        return 0

    lax.fori_loop(0, 4, per_block, 0)

    @pl.when(has_prev & (c == 1))
    def _():
        hand_full.wait_recv()
        sl[...] = (away[blocks(PROMPT + 2, 4), :].astype(F32) + bufs[...].astype(F32)).astype(BF)
        back.start()

    @pl.when(has_prev & (c == 0))
    def _():
        hand_half.wait_recv()
        sl[0:2 * BLK, :] = away[blocks(PROMPT + 2, 2), :]
        sl[2 * BLK:, :] = (away[blocks(PROMPT + 4, 2), :].astype(F32) + bufs[0:2 * BLK].astype(F32)).astype(BF)
        back.start()

    for h in order:
        cp_a(1 - y, h).wait_recv()
        sa[half(h), :] = (away[rows(2 * (1 - y) + c, h), :].astype(F32)
                          + bufa[1 - y, half(h), :].astype(F32)).astype(BF)
        cp_b(h).start()

    for step, h in enumerate(order):
        cp_a(y, h).wait_recv()
        tot[half(h), :] = away[rows(2 * y + c, h), :].astype(F32) + bufa[y, half(h), :].astype(F32)
        cp_b(h).wait_recv()
        tot[half(h), :] += bufb[half(h), :].astype(F32)

        @pl.when(z == 2)
        def _(h=h):
            sb[half(h), :] = tot[half(h), :].astype(BF)
            cp_c(h, 0, 1 + 2 * h).start()

        @pl.when((z == 1) | (z == 3))
        def _(h=h, step=step):
            if step == 1:
                cp_c(h, 0, 0).wait_recv()
                tot[half(h), :] += bufc[0, half(h), :].astype(F32)
            sb[half(h), :] = tot[half(h), :].astype(BF)
            cp_c(h, (z - 1) // 2, 0).start()

    @pl.when(z == 0)
    def _():
        for h in order:
            for slot in (0, 1):
                cp_c(h, slot, 1).wait_recv()
                tot[half(h), :] += bufc[slot, half(h), :].astype(F32)
        tot[:, 0:BLK] += dk_ref[OWN * BLK:, :]
        tot[:, BLK:2 * BLK] += dv_ref[OWN * BLK:, :]

    @pl.when(z != 0)
    def _():
        tot[:, 0:BLK] = dk_ref[OWN * BLK:, :]
        tot[:, BLK:2 * BLK] = dv_ref[OWN * BLK:, :]

    @pl.when(from_next)
    def _():
        back.wait_recv()
        tot[...] += bufl[0].astype(F32)

    @pl.when(gets_near)
    def _():
        near_back.wait_recv()
        tot[...] += bufl[1].astype(F32)

    @pl.when(gets_far)
    def _():
        far_back.wait_recv()
        tot[2 * BLK:, :] += bufl[2, 0:2 * BLK].astype(F32)

    x = k_ref[...].astype(F32)
    r = lax.rsqrt(jnp.mean(x * x, axis=-1, keepdims=True) + 1e-6)
    unit = x * r
    dk = tot[:, 0:BLK] * SCALE
    both = dk * unit
    gown[...] = jnp.zeros_like(gown)
    gown[0:1, :] = jnp.sum(qpart[...], axis=0, keepdims=True)
    gown[1:2, :] = jnp.sum(both, axis=0, keepdims=True)
    cg = [copy_to(gown, gall.at[me], send_g.at[o - 1], recv_g.at[me], dp, lax.rem(me + o, 16)) for o in range(1, 16)]
    for q in cg:
        q.start()
    gall[me] = gown[...]
    kgain = kg_ref[...]
    mean = jnp.mean(both * kgain, axis=-1, keepdims=True)
    gk_ref[...] = (r * (dk * kgain - unit * mean)).astype(BF)
    gv_ref[...] = tot[:, BLK:2 * BLK].astype(BF)
    for o in range(1, 16):
        p = lax.rem(me + o, 16)
        copy_to(gown, gall.at[p], send_g.at[o - 1], recv_g.at[p], dp, p).wait_recv()
    total = gall[0]
    for o in range(1, 16):
        total = total + gall[o]
    for q in cg:
        q.wait_send()
    gown[...] = total
    ch = [copy_to(gown, gdp.at[dp], send_g.at[14 + o], recv_g.at[16 + dp], lax.rem(dp + o, 8), me) for o in range(1, 8)]
    for q in ch:
        q.start()
    gdp[dp] = total
    for o in range(1, 8):
        p = lax.rem(dp + o, 8)
        copy_to(gown, gdp.at[p], send_g.at[14 + o], recv_g.at[16 + p], p, me).wait_recv()
    total = gdp[0]
    for o in range(1, 8):
        total = total + gdp[o]
    gain_ref[...] = total
    for q in ch:
        q.wait_send()
    for h in (0, 1):
        cp_a(0, h).wait_send()
        cp_a(1, h).wait_send()
        cp_b(h).wait_send()

    @pl.when(z != 0)
    def _():
        for h in (0, 1):
            cp_c(h, 0, 0).wait_send()

    @pl.when(has_prev & (c == 0))
    def _():
        hand_full.wait_send()

    @pl.when(has_prev & (c == 1))
    def _():
        hand_half.wait_send()

    @pl.when(has_prev)
    def _():
        back.wait_send()

    @pl.when(sends_near)
    def _():
        near_back.wait_send()

    @pl.when(sends_far)
    def _():
        far_back.wait_send()

    @pl.when(z == 0)
    def _():
        for k in range(4):
            kv_z(0, 1, k).wait_send()

    @pl.when((z == 1) | (z == 3))
    def _():
        kv_z(0, 1, 0).wait_send()

    for h in (0, 1):
        kv_y(h).wait_send()
        kv_s(0, h).wait_send()
        kv_s(1, h).wait_send()

    @pl.when((c == 0) & (n >= 2))
    def _():
        own_sib.wait_send()

    @pl.when(has_next)
    def _():
        ahead.wait_send()

    @pl.when(sends_kfar)
    def _():
        kfar.wait_send()

    @pl.when(has_prev & (c == 1))
    def _():
        relay_full.wait_send()

    @pl.when(has_prev & (c == 0))
    def _():
        relay_half.wait_send()


def fused(lens, frm, qg, kg, q, do, k, v):
    dma = pltpu.SemaphoreType.DMA
    rows = SLOTS * BLK
    tiles = 4096 // RT
    pair = pltpu.VMEM((GRP, 2 * BLK), BF)
    two = pltpu.VMEM((2, GRP, 2 * BLK), BF)
    return pl.pallas_call(
        fused_kernel,
        out_shape=(
            jax.ShapeDtypeStruct((512, 1024), BF),
            jax.ShapeDtypeStruct((GRP, BLK), BF),
            jax.ShapeDtypeStruct((GRP, BLK), BF),
            jax.ShapeDtypeStruct((8, BLK), F32),
        ),
        in_specs=[SM, SM, VM, VM, VM, VM, VM, VM],
        out_specs=(VM, VM, VM, VM),
        scratch_shapes=[
            pltpu.VMEM((rows, 2 * BLK), BF),
            pltpu.VMEM((tiles, RT, BLK), BF),
            pltpu.VMEM((tiles, BLK, RT), BF),
            pltpu.VMEM((tiles, RT, BLK), BF),
            pltpu.VMEM((tiles, BLK, RT), BF),
            pltpu.VMEM((SLOTS, BLK, BLK), BF),
            pltpu.VMEM((POS, BLK, RT), F32),
            pltpu.VMEM((POS, BLK, RT), F32),
            pltpu.VMEM((POS, 8, RT), F32),
            pltpu.VMEM((POS, 8, RT), F32),
            pltpu.VMEM((POS, 8, RT), F32),
            pltpu.VMEM((BLK, RT), F32),
            pltpu.VMEM((rows, BLK), F32),
            pltpu.VMEM((rows, BLK), F32),
            pltpu.VMEM((8, BLK), F32),
            pltpu.VMEM((OWN * BLK, 2 * BLK), BF),
            two, pair, two, pltpu.VMEM((3, GRP, 2 * BLK), BF), pair, pair, pair, pair,
            pltpu.VMEM((GRP, 2 * BLK), F32),
            pltpu.VMEM((8, BLK), F32),
            pltpu.VMEM((16, 8, BLK), F32),
            pltpu.VMEM((8, 8, BLK), F32),
        ] + [dma((m,)) for m in (4, 2, 2, 2, 4, 4, 5, 3, 4, 4, 2, 2, 2, 4, 5, 4, 22, 24)],
        compiler_params=pltpu.CompilerParams(
            collective_id=0, has_side_effects=True, vmem_limit_bytes=60 * 1024 * 1024),
    )(lens, frm, qg, kg, q, do, k, v)


PIECES = 4


def hand_out_kernel(gains_ref, gq_ref, gk_ref, gv_ref, oq_ref, ok_ref, ov_ref, gq_gain_ref, gk_gain_ref,
                    bq, bk, bv, sin, sout):
    step = bq.shape[0] // PIECES
    legs = [(gq_ref.at[pl.ds(j * step, step)], bq.at[pl.ds(j * step, step)], oq_ref.at[pl.ds(j * step, step)])
            for j in range(PIECES)]
    legs += [(gk_ref, bk, ok_ref), (gv_ref, bv, ov_ref)]
    into = [pltpu.make_async_copy(x, m, sin.at[j]) for j, (x, m, _) in enumerate(legs)]
    out = [pltpu.make_async_copy(m, o, sout.at[j]) for j, (_, m, o) in enumerate(legs)]
    for copy in into:
        copy.start()
    gq_gain_ref[...] = gains_ref[0, :]
    gk_gain_ref[...] = gains_ref[1, :]
    for j in range(len(legs)):
        into[j].wait()
        out[j].start()
    for copy in out:
        copy.wait()


def hand_out(gains, gq, gk, gv):
    anywhere = pl.BlockSpec(memory_space=pl.ANY)
    flat = jax.ShapeDtypeStruct((BLK,), F32)
    dma = pltpu.SemaphoreType.DMA
    return pl.pallas_call(
        hand_out_kernel,
        out_shape=tuple(jax.ShapeDtypeStruct(t.shape, t.dtype) for t in (gq, gk, gv)) + (flat, flat),
        in_specs=[VM, anywhere, anywhere, anywhere],
        out_specs=(anywhere, anywhere, anywhere, VM, VM),
        scratch_shapes=[pltpu.VMEM(t.shape, t.dtype) for t in (gq, gk, gv)] + [dma((PIECES + 2,)), dma((PIECES + 2,))],
    )(gains, gq, gk, gv)


def body(q_raw, k_raw, values, d_out, q_gain, k_gain, resp_len, block_parent, block_from):
    gq, gk, gv, gains = fused(resp_len[0], block_from[0], q_gain.reshape(1, BLK), k_gain.reshape(1, BLK),
                              q_raw[0], d_out[0], k_raw[0], values[0])
    gq, gk, gv, q_gain_grad, k_gain_grad = hand_out(gains, gq, gk, gv)
    return gq[None], gk[None], gv[None], q_gain_grad, k_gain_grad


def solution(mesh):
    tok = P("dp", "ctx", None)
    return jax.shard_map(
        body,
        mesh=mesh,
        in_specs=(tok, tok, tok, tok, P(), P(), P("dp", None), P("dp", None), P("dp", "ctx")),
        out_specs=(tok, tok, tok, P(), P()),
        check_vma=False,
    )
```

time: 171 us -> 122 us (0.71)
  Pallas kernels: 165 us -> 121 us
  local copies, waits for them, and re-layouts: 5.02 us -> 0 us
    pallas_call x3 -> x2, Pallas kernels: 165 us -> 121 us  [the longest x1 117 us: fused(): pl.pallas_call(fused_kernel, out_shape=(jax.ShapeDtypeStruct((512, 1024),...]
    unnamed x12 -> x0, local copies, waits for them, and re-layouts: 4.5 us -> none
where the time goes in v2:
time: 122 us; the launch traced here: 121 us
  Pallas kernels  121 us (99%)
    pallas_call x1, Pallas kernels, fused(): pl.pallas_call(fused_kernel, out_shape=(jax.ShapeDtypeStruct((512, 1024),...  117 us
    pallas_call x1, Pallas kernels, hand_out(): pl.pallas_call(hand_out_kernel, out_shape=tuple((jax.ShapeDtypeStruct(t.s...  3.29 us

profile of v2, /device:TPU:1, one launch (start us, length us, event | category | flops | bytes accessed | tf_op | source)
XLA Modules:
  0.0 121.4 jit_solution(3368792902342639266)
XLA Ops:
  0.6 117.5 %shard_map.119 = (bf16[512,1024]{1,0:T(8,128)(2,1)}, bf16[512,128]{1,0:T(8,128)(2,1)}, bf16[512,128]{1,0:T(8,128)(2,1)}, f32[8,128]{1,0:T(8,128)}) custom-call(s32[8]{0:T(128)} %bitcast.15, s32[4]{0:T(128)} %bitcast.16, f32[1,128]{1,0:T(1,128)} %bitcast.17, f32[1,128]{1,0:T(1,128)} %bitcast.18, bf16[512,1024]{1,0:T(8,128)(2,1)} %bitcast.11, ...), custom_call_target="tpu_custom_call" | custom-call | tf_op jit(solution)/shard_map/pallas_call | solution.py:642
  118.1 3.3 %shard_map.120 = (bf16[512,1024]{1,0:T(8,128)(2,1)}, bf16[512,128]{1,0:T(8,128)(2,1)}, bf16[512,128]{1,0:T(8,128)(2,1)}, f32[128]{0:T(128)}, f32[128]{0:T(128)}) custom-call(f32[8,128]{1,0:T(8,128)} %get-tuple-element.14.gains_ref, bf16[512,1024]{1,0:T(8,128)(2,1)} %get-tuple-element.15.gq_ref, bf16[512,128]{1,0:T(8,128)(2,1)} %get-tuple-element.16.gk_ref, ...), custom_call_target="tpu_custom_call" | custom-call | tf_op jit(solution)/shard_map/pallas_call | solution.py:706

commit v3 on v2

--- a/solution.py
+++ b/solution.py
@@ -64,7 +64,7 @@
 def fused_kernel(len_ref, from_ref, qg_ref, kg_ref, q_ref, do_ref, k_ref, v_ref,
                  gq_ref, gk_ref, gv_ref, gain_ref,
                  kv_ref, qn, qt, dn, dt, kt, w_s, dp_s, m_s, s_s, f_s, dq_s, dk_ref, dv_ref, qpart,
-                 away, bufa, bufb, bufc, bufl, bufs, sa, sb, sl, tot, gown, gall, gdp,
+                 away, bufa, bufb, bufc, bufl, bufs, sa, sb, sl, tot, gown, gsum, gall, gdp,
                  send_z, recv_z, send_y, recv_y, send_s, recv_s, fsend_l, frecv_l,
                  send_a, recv_a, send_b, recv_b, send_c, recv_c, send_l, recv_l, send_g, recv_g):
     dp = lax.axis_index("dp")
@@ -140,6 +140,7 @@
 
     early = jnp.where(z == 1, 1, 0)
     order = (early, 1 - early)
+    sums = (dv_ref, dk_ref)
 
     def half(h):
         return pl.ds(pl.multiple_of(h * 256, 256), 256)
@@ -147,55 +148,154 @@
     def rows(g, h):
         return pl.ds(pl.multiple_of(g * GRP + h * 256, 256), 256)
 
+    def group(g):
+        return pl.ds(pl.multiple_of(g * GRP, GRP), GRP)
+
     def blocks(first, count):
         return pl.ds(first * BLK, count * BLK)
 
-    def cp_a(j, h):
-        return copy_to(away.at[rows(2 * j + 1 - c, h)], bufa.at[j, half(h)],
-                       send_a.at[2 * j + h], recv_a.at[2 * j + h], dp, sib)
-
-    def cp_b(h):
-        return copy_to(sa.at[half(h)], bufb.at[half(h)], send_b.at[h], recv_b.at[h], dp, yny)
-
-    def cp_c(h, slot, zz):
-        return copy_to(sb.at[half(h)], bufc.at[slot, half(h)], send_c.at[h], recv_c.at[2 * slot + h],
-                       dp, zz * 4 + 2 * y + c)
-
-    has_prev = n >= 3
+    def cp_a(x, j):
+        return copy_to(away.at[x, group(2 * j + 1 - c)], bufa.at[x, j],
+                       send_a.at[2 * x + j], recv_a.at[2 * x + j], dp, sib)
+
+    def cp_b(x, h):
+        return copy_to(sa.at[x, half(h)], bufb.at[x, half(h)], send_b.at[2 * x + h], recv_b.at[2 * x + h], dp, yny)
+
+    def cp_c(x, h, slot, zz):
+        return copy_to(sb.at[x, half(h)], bufc.at[slot, x, half(h)], send_c.at[2 * x + h],
+                       recv_c.at[4 * slot + 2 * x + h], dp, zz * 4 + 2 * y + c)
+
     from_next = (n >= 2) & (n + 1 <= 7)
-    hand_full = copy_to(away.at[blocks(PROMPT + 6, 4)], bufs, send_l.at[0], recv_l.at[0], dp, sib)
-    hand_half = copy_to(away.at[blocks(PROMPT, 2)], bufs.at[pl.ds(0, 2 * BLK)], send_l.at[1], recv_l.at[0], dp, sib)
-    back = copy_to(sl, bufl.at[0], send_l.at[2], recv_l.at[1], dp, lax.rem(me + 14, 16))
-    near_back = copy_to(away.at[blocks(PROMPT + 6, 4)], bufl.at[1], send_l.at[3], recv_l.at[2], dp, sib)
-    far_back = copy_to(away.at[blocks(PROMPT, 2)], bufl.at[2, pl.ds(0, 2 * BLK)], send_l.at[4], recv_l.at[3],
-                       dp, lax.rem(me + 13, 16))
     sends_near = (c == 1) & (n >= 2)
     gets_near = (c == 0) & (n >= 2)
     sends_far = (c == 0) & (n >= 4)
     gets_far = (c == 1) & (n >= 2) & (n + 2 <= 7)
-
-    def hand_over(s, _):
-        rr = pl.ds(pl.multiple_of(s * BLK, BLK), BLK)
-        away[rr, 0:BLK] = dk_ref[rr, :].astype(BF)
-        away[rr, BLK:2 * BLK] = dv_ref[rr, :].astype(BF)
-        return 0
-
-    def local_sends():
+    two_blocks = pl.ds(0, 2 * BLK)
+
+    def leg(src, dst, k, x, to):
+        return copy_to(src, dst, send_l.at[2 * k + x], recv_l.at[2 * k + x], dp, to)
+
+    def hand_full(x):
+        return leg(away.at[x, blocks(PROMPT + 6, 4)], bufs.at[x], 0, x, sib)
+
+    def hand_half(x):
+        return leg(away.at[x, blocks(PROMPT, 2)], bufs.at[x, two_blocks], 0, x, sib)
+
+    def back(x):
+        return leg(sl.at[x], bufl.at[0, x], 1, x, lax.rem(me + 14, 16))
+
+    def near_back(x):
+        return leg(away.at[x, blocks(PROMPT + 6, 4)], bufl.at[1, x], 2, x, sib)
+
+    def far_back(x):
+        return leg(away.at[x, blocks(PROMPT, 2)], bufl.at[2, x, two_blocks], 3, x, lax.rem(me + 13, 16))
+
+    def hand_over(x, lo, hi):
+        def one(s, _):
+            rr = pl.ds(pl.multiple_of(s * BLK, BLK), BLK)
+            away[x, rr, :] = sums[x][rr, :].astype(BF)
+            return 0
+
+        lax.fori_loop(lo, hi, one, 0)
+
+    def local_start(x):
         @pl.when(has_prev & (c == 0))
         def _():
-            hand_full.start()
+            hand_full(x).start()
 
         @pl.when(has_prev & (c == 1))
         def _():
-            hand_half.start()
+            hand_half(x).start()
 
         @pl.when(sends_near)
         def _():
-            near_back.start()
+            near_back(x).start()
 
         @pl.when(sends_far)
         def _():
-            far_back.start()
+            far_back(x).start()
+
+    def local_mid(x):
+        @pl.when(has_prev & (c == 1))
+        def _():
+            hand_full(x).wait_recv()
+            sl[x] = (away[x, blocks(PROMPT + 2, 4), :].astype(F32) + bufs[x].astype(F32)).astype(BF)
+            back(x).start()
+
+        @pl.when(has_prev & (c == 0))
+        def _():
+            hand_half(x).wait_recv()
+            sl[x, 0:2 * BLK, :] = away[x, blocks(PROMPT + 2, 2), :]
+            sl[x, 2 * BLK:, :] = (away[x, blocks(PROMPT + 4, 2), :].astype(F32)
+                                  + bufs[x, 0:2 * BLK].astype(F32)).astype(BF)
+            back(x).start()
+
+    def local_end(x):
+        @pl.when(from_next)
+        def _():
+            back(x).wait_recv()
+            tot[x] += bufl[0, x].astype(F32)
+
+        @pl.when(gets_near)
+        def _():
+            near_back(x).wait_recv()
+            tot[x] += bufl[1, x].astype(F32)
+
+        @pl.when(gets_far)
+        def _():
+            far_back(x).wait_recv()
+            tot[x, 2 * BLK:, :] += bufl[2, x, 0:2 * BLK].astype(F32)
+
+    def stage_b(x):
+        cp_a(x, 1 - y).wait_recv()
+        for h in order:
+            sa[x, half(h), :] = (away[x, rows(2 * (1 - y) + c, h), :].astype(F32)
+                                 + bufa[x, 1 - y, half(h), :].astype(F32)).astype(BF)
+            cp_b(x, h).start()
+
+    def stage_c(x):
+        cp_a(x, y).wait_recv()
+        for step, h in enumerate(order):
+            tot[x, half(h), :] = (away[x, rows(2 * y + c, h), :].astype(F32)
+                                  + bufa[x, y, half(h), :].astype(F32))
+            cp_b(x, h).wait_recv()
+            tot[x, half(h), :] += bufb[x, half(h), :].astype(F32)
+
+            @pl.when(z == 2)
+            def _(h=h):
+                sb[x, half(h), :] = tot[x, half(h), :].astype(BF)
+                cp_c(x, h, 0, 1 + 2 * h).start()
+
+            if step == 0:
+                @pl.when((z == 1) | (z == 3))
+                def _(h=h):
+                    sb[x, half(h), :] = tot[x, half(h), :].astype(BF)
+                    cp_c(x, h, (z - 1) // 2, 0).start()
+
+    def stage_d(x):
+        h = 1 - early
+
+        @pl.when((z == 1) | (z == 3))
+        def _():
+            cp_c(x, h, 0, 0).wait_recv()
+            tot[x, half(h), :] += bufc[0, x, half(h), :].astype(F32)
+            sb[x, half(h), :] = tot[x, half(h), :].astype(BF)
+            cp_c(x, h, (z - 1) // 2, 0).start()
+
+    def stage_e(x):
+        own = sums[x][OWN * BLK:, :]
+
+        @pl.when(z != 0)
+        def _():
+            tot[x] = own
+
+        @pl.when(z == 0)
+        def _():
+            tot[x] += own
+            for h in order:
+                for slot in (0, 1):
+                    cp_c(x, h, slot, 1).wait_recv()
+                    tot[x, half(h), :] += bufc[slot, x, half(h), :].astype(F32)
 
     dk_ref[...] = jnp.zeros_like(dk_ref)
     dv_ref[...] = jnp.zeros_like(dv_ref)
@@ -302,19 +402,23 @@
             g = (2 * y + 1 - c) if j == 0 else (2 * (1 - y) + 1 - c)
             copy_to(krows(g, h), krows(g, h), send_s.at[2 * j + h], recv_s.at[2 * j + h], dp, sib).wait_recv()
 
-    @pl.when(((c == 1) & (n >= 2)) | ((c == 0) & has_prev))
-    def _():
-        own_sib.wait_recv()
-
-    @pl.when(gets_kfar | ((c == 1) & has_prev))
-    def _():
-        kfar.wait_recv()
-
     def slot_t(s, _):
         kt[s] = kv_ref[pl.ds(pl.multiple_of(s * BLK, BLK), BLK), 0:BLK].T
         return 0
 
-    lax.fori_loop(0, SLOTS, slot_t, 0)
+    lax.fori_loop(0, PROMPT, slot_t, 0)
+    lax.fori_loop(OWN, SLOTS, slot_t, 0)
+
+    def local_arrive():
+        @pl.when(((c == 1) & (n >= 2)) | ((c == 0) & has_prev))
+        def _():
+            own_sib.wait_recv()
+
+        @pl.when(gets_kfar | ((c == 1) & has_prev))
+        def _():
+            kfar.wait_recv()
+
+        lax.fori_loop(PROMPT, OWN, slot_t, 0)
 
     def per_block(i, _):
         b, off, live = facts(i)
@@ -359,8 +463,10 @@
                             m_s[pos + u, :, cs] = jnp.where(seen(pos + u), m, LOW)
                         w_s[pos + u, :, cs] = w.reshape(BLK, CS)
 
-            def over(body, init):
+            def over(body, init, between=None):
                 init = lax.fori_loop(0, pc, lambda c, x: body(c * CBP, CBP, False, x), init)
+                if between is not None:
+                    between()
                 init = lax.fori_loop(lc, REACH // CBL, lambda c, x: body(PROMPT + c * CBL, CBL, False, x), init)
                 return body(POS - 1, 1, True, init)
 
@@ -368,7 +474,12 @@
                 first_pass(pos, nb, diag)
                 return x
 
-            over(p1, 0)
+            def await_local():
+                @pl.when(i == 0)
+                def _():
+                    local_arrive()
+
+            over(p1, 0, await_local)
             m = m_s[...]
             top = jnp.max(jnp.max(m, axis=0), axis=0, keepdims=True)
             f = jnp.exp2(m - top[None])
@@ -401,6 +512,13 @@
                 return jnp.concatenate(accs, axis=1)
 
             delta = over(p3, jnp.zeros((8, RT), F32))
+            @pl.when(i == 3)
+            def _():
+                hand_over(0, 0, OWN)
+                for j in (0, 1):
+                    cp_a(0, j).start()
+                local_start(0)
+
             delta = jnp.sum(delta, axis=0, keepdims=True)
             qrows = qn[t]
 
@@ -424,23 +542,31 @@
 
             @pl.when(i == 3)
             def _():
-                lax.fori_loop(PROMPT, OWN, hand_over, 0)
-                local_sends()
-
-            def p4_prompt(j, _):
-                @pl.when(j < pc)
-                def _():
-                    p4(j * CBP, CBP, False, 0)
-
-                @pl.when(i == 3)
-                def _():
-                    lax.fori_loop(8 * j, 8 * j + 8, hand_over, 0)
-                    for h in order:
-                        cp_a(j, h).start()
-
-                return 0
-
-            lax.fori_loop(0, 2, p4_prompt, 0)
+                hand_over(1, PROMPT, OWN)
+                local_start(1)
+                stage_b(0)
+                local_mid(0)
+
+            @pl.when(0 < pc)
+            def _():
+                p4(0, CBP, False, 0)
+
+            @pl.when(i == 3)
+            def _():
+                hand_over(1, 0, 8)
+                cp_a(1, 0).start()
+                stage_c(0)
+
+            @pl.when(1 < pc)
+            def _():
+                p4(CBP, CBP, False, 0)
+
+            @pl.when(i == 3)
+            def _():
+                hand_over(1, 8, PROMPT)
+                cp_a(1, 1).start()
+                stage_d(0)
+
             dqt = dq_s[...]
             dq = dqt.T * SCALE
             rows = pl.ds(pl.multiple_of(i * BLK, BLK), BLK)
@@ -463,140 +589,87 @@
 
     lax.fori_loop(0, 4, per_block, 0)
 
-    @pl.when(has_prev & (c == 1))
-    def _():
-        hand_full.wait_recv()
-        sl[...] = (away[blocks(PROMPT + 2, 4), :].astype(F32) + bufs[...].astype(F32)).astype(BF)
-        back.start()
-
-    @pl.when(has_prev & (c == 0))
-    def _():
-        hand_half.wait_recv()
-        sl[0:2 * BLK, :] = away[blocks(PROMPT + 2, 2), :]
-        sl[2 * BLK:, :] = (away[blocks(PROMPT + 4, 2), :].astype(F32) + bufs[0:2 * BLK].astype(F32)).astype(BF)
-        back.start()
-
-    for h in order:
-        cp_a(1 - y, h).wait_recv()
-        sa[half(h), :] = (away[rows(2 * (1 - y) + c, h), :].astype(F32)
-                          + bufa[1 - y, half(h), :].astype(F32)).astype(BF)
-        cp_b(h).start()
-
-    for step, h in enumerate(order):
-        cp_a(y, h).wait_recv()
-        tot[half(h), :] = away[rows(2 * y + c, h), :].astype(F32) + bufa[y, half(h), :].astype(F32)
-        cp_b(h).wait_recv()
-        tot[half(h), :] += bufb[half(h), :].astype(F32)
-
-        @pl.when(z == 2)
-        def _(h=h):
-            sb[half(h), :] = tot[half(h), :].astype(BF)
-            cp_c(h, 0, 1 + 2 * h).start()
-
-        @pl.when((z == 1) | (z == 3))
-        def _(h=h, step=step):
-            if step == 1:
-                cp_c(h, 0, 0).wait_recv()
-                tot[half(h), :] += bufc[0, half(h), :].astype(F32)
-            sb[half(h), :] = tot[half(h), :].astype(BF)
-            cp_c(h, (z - 1) // 2, 0).start()
-
-    @pl.when(z == 0)
-    def _():
-        for h in order:
-            for slot in (0, 1):
-                cp_c(h, slot, 1).wait_recv()
-                tot[half(h), :] += bufc[slot, half(h), :].astype(F32)
-        tot[:, 0:BLK] += dk_ref[OWN * BLK:, :]
-        tot[:, BLK:2 * BLK] += dv_ref[OWN * BLK:, :]
-
-    @pl.when(z != 0)
-    def _():
-        tot[:, 0:BLK] = dk_ref[OWN * BLK:, :]
-        tot[:, BLK:2 * BLK] = dv_ref[OWN * BLK:, :]
-
-    @pl.when(from_next)
-    def _():
-        back.wait_recv()
-        tot[...] += bufl[0].astype(F32)
-
-    @pl.when(gets_near)
-    def _():
-        near_back.wait_recv()
-        tot[...] += bufl[1].astype(F32)
-
-    @pl.when(gets_far)
-    def _():
-        far_back.wait_recv()
-        tot[2 * BLK:, :] += bufl[2, 0:2 * BLK].astype(F32)
-
-    x = k_ref[...].astype(F32)
-    r = lax.rsqrt(jnp.mean(x * x, axis=-1, keepdims=True) + 1e-6)
-    unit = x * r
-    dk = tot[:, 0:BLK] * SCALE
-    both = dk * unit
+    def key_part(k, acc):
+        rr = pl.ds(pl.multiple_of(k * BLK, BLK), BLK)
+        both = dk_ref[rr, :] * kv_ref[rr, 0:BLK].astype(F32)
+        return acc + jnp.sum(both.reshape(BLK // 8, 8, BLK), axis=0)
+
+    kpart = lax.fori_loop(0, SLOTS, key_part, jnp.zeros((8, BLK), F32))
+    kgain = kg_ref[...]
     gown[...] = jnp.zeros_like(gown)
     gown[0:1, :] = jnp.sum(qpart[...], axis=0, keepdims=True)
-    gown[1:2, :] = jnp.sum(both, axis=0, keepdims=True)
+    gown[1:2, :] = jnp.sum(kpart, axis=0, keepdims=True) * SCALE / kgain
     cg = [copy_to(gown, gall.at[me], send_g.at[o - 1], recv_g.at[me], dp, lax.rem(me + o, 16)) for o in range(1, 16)]
+    ch = [copy_to(gsum, gdp.at[dp], send_g.at[14 + o], recv_g.at[16 + dp], lax.rem(dp + o, 8), me) for o in range(1, 8)]
     for q in cg:
         q.start()
     gall[me] = gown[...]
-    kgain = kg_ref[...]
-    mean = jnp.mean(both * kgain, axis=-1, keepdims=True)
-    gk_ref[...] = (r * (dk * kgain - unit * mean)).astype(BF)
-    gv_ref[...] = tot[:, BLK:2 * BLK].astype(BF)
+    stage_b(1)
+    stage_e(0)
+    for h in (0, 1):
+        cp_b(1, h).wait_send()
+    local_mid(1)
+    stage_c(1)
     for o in range(1, 16):
         p = lax.rem(me + o, 16)
         copy_to(gown, gall.at[p], send_g.at[o - 1], recv_g.at[p], dp, p).wait_recv()
     total = gall[0]
     for o in range(1, 16):
         total = total + gall[o]
-    for q in cg:
-        q.wait_send()
-    gown[...] = total
-    ch = [copy_to(gown, gdp.at[dp], send_g.at[14 + o], recv_g.at[16 + dp], lax.rem(dp + o, 8), me) for o in range(1, 8)]
+    gsum[...] = total
     for q in ch:
         q.start()
     gdp[dp] = total
+    local_end(0)
+    gv_ref[...] = tot[0].astype(BF)
+    stage_d(1)
+    stage_e(1)
+    local_end(1)
+    x = k_ref[...].astype(F32)
+    r = lax.rsqrt(jnp.mean(x * x, axis=-1, keepdims=True) + 1e-6)
+    unit = x * r
+    dk = tot[1] * SCALE
+    mean = jnp.mean(dk * unit * kgain, axis=-1, keepdims=True)
+    gk_ref[...] = (r * (dk * kgain - unit * mean)).astype(BF)
     for o in range(1, 8):
         p = lax.rem(dp + o, 8)
-        copy_to(gown, gdp.at[p], send_g.at[14 + o], recv_g.at[16 + p], p, me).wait_recv()
+        copy_to(gsum, gdp.at[p], send_g.at[14 + o], recv_g.at[16 + p], p, me).wait_recv()
     total = gdp[0]
     for o in range(1, 8):
         total = total + gdp[o]
     gain_ref[...] = total
-    for q in ch:
+    for q in cg + ch:
         q.wait_send()
-    for h in (0, 1):
-        cp_a(0, h).wait_send()
-        cp_a(1, h).wait_send()
-        cp_b(h).wait_send()
-
-    @pl.when(z != 0)
-    def _():
+    for x in (0, 1):
         for h in (0, 1):
-            cp_c(h, 0, 0).wait_send()
-
-    @pl.when(has_prev & (c == 0))
-    def _():
-        hand_full.wait_send()
-
-    @pl.when(has_prev & (c == 1))
-    def _():
-        hand_half.wait_send()
-
-    @pl.when(has_prev)
-    def _():
-        back.wait_send()
-
-    @pl.when(sends_near)
-    def _():
-        near_back.wait_send()
-
-    @pl.when(sends_far)
-    def _():
-        far_back.wait_send()
+            cp_a(x, h).wait_send()
+            if x == 0:
+                cp_b(x, h).wait_send()
+
+        @pl.when(z != 0)
+        def _(x=x):
+            for h in (0, 1):
+                cp_c(x, h, 0, 0).wait_send()
+
+        @pl.when(has_prev & (c == 0))
+        def _(x=x):
+            hand_full(x).wait_send()
+
+        @pl.when(has_prev & (c == 1))
+        def _(x=x):
+            hand_half(x).wait_send()
+
+        @pl.when(has_prev)
+        def _(x=x):
+            back(x).wait_send()
+
+        @pl.when(sends_near)
+        def _(x=x):
+            near_back(x).wait_send()
+
+        @pl.when(sends_far)
+        def _(x=x):
+            far_back(x).wait_send()
 
     @pl.when(z == 0)
     def _():
@@ -637,8 +710,8 @@
     dma = pltpu.SemaphoreType.DMA
     rows = SLOTS * BLK
     tiles = 4096 // RT
-    pair = pltpu.VMEM((GRP, 2 * BLK), BF)
-    two = pltpu.VMEM((2, GRP, 2 * BLK), BF)
+    pair = pltpu.VMEM((2, GRP, BLK), BF)
+    two = pltpu.VMEM((2, 2, GRP, BLK), BF)
     return pl.pallas_call(
         fused_kernel,
         out_shape=(
@@ -665,13 +738,14 @@
             pltpu.VMEM((rows, BLK), F32),
             pltpu.VMEM((rows, BLK), F32),
             pltpu.VMEM((8, BLK), F32),
-            pltpu.VMEM((OWN * BLK, 2 * BLK), BF),
-            two, pair, two, pltpu.VMEM((3, GRP, 2 * BLK), BF), pair, pair, pair, pair,
-            pltpu.VMEM((GRP, 2 * BLK), F32),
+            pltpu.VMEM((2, OWN * BLK, BLK), BF),
+            two, pair, two, pltpu.VMEM((3, 2, GRP, BLK), BF), pair, pair, pair, pair,
+            pltpu.VMEM((2, GRP, BLK), F32),
+            pltpu.VMEM((8, BLK), F32),
             pltpu.VMEM((8, BLK), F32),
             pltpu.VMEM((16, 8, BLK), F32),
             pltpu.VMEM((8, 8, BLK), F32),
-        ] + [dma((m,)) for m in (4, 2, 2, 2, 4, 4, 5, 3, 4, 4, 2, 2, 2, 4, 5, 4, 22, 24)],
+        ] + [dma((m,)) for m in (4, 2, 2, 2, 4, 4, 5, 3, 4, 4, 4, 4, 4, 8, 8, 8, 22, 24)],
         compiler_params=pltpu.CompilerParams(
             collective_id=0, has_side_effects=True, vmem_limit_bytes=60 * 1024 * 1024),
     )(lens, frm, qg, kg, q, do, k, v)

time: 122 us -> 109 us (0.89)
  Pallas kernels: 121 us -> 108 us
    pallas_call x1, Pallas kernels: 117 us -> 105 us  [fused(): pl.pallas_call(fused_kernel, out_shape=(jax.ShapeDtypeStruct((512, 1024),...]
where the time goes in v3:
time: 109 us
  Pallas kernels  108 us (99%)
    pallas_call x1, Pallas kernels, fused(): pl.pallas_call(fused_kernel, out_shape=(jax.ShapeDtypeStruct((512, 1024),...  105 us
    pallas_call x1, Pallas kernels, hand_out(): pl.pallas_call(hand_out_kernel, out_shape=tuple((jax.ShapeDtypeStruct(t.s...  3.29 us

profile of v3, /device:TPU:1, one launch (start us, length us, event | category | flops | bytes accessed | tf_op | source)
XLA Modules:
  0.0 108.5 jit_solution(13671134892147175467)
XLA Ops:
  0.6 104.6 %shard_map.119 = (bf16[512,1024]{1,0:T(8,128)(2,1)}, bf16[512,128]{1,0:T(8,128)(2,1)}, bf16[512,128]{1,0:T(8,128)(2,1)}, f32[8,128]{1,0:T(8,128)}) custom-call(s32[8]{0:T(128)} %bitcast.15, s32[4]{0:T(128)} %bitcast.16, f32[1,128]{1,0:T(1,128)} %bitcast.17, f32[1,128]{1,0:T(1,128)} %bitcast.18, bf16[512,1024]{1,0:T(8,128)(2,1)} %bitcast.11, ...), custom_call_target="tpu_custom_call" | custom-call | tf_op jit(solution)/shard_map/pallas_call | solution.py:715
  105.2 3.3 %shard_map.120 = (bf16[512,1024]{1,0:T(8,128)(2,1)}, bf16[512,128]{1,0:T(8,128)(2,1)}, bf16[512,128]{1,0:T(8,128)(2,1)}, f32[128]{0:T(128)}, f32[128]{0:T(128)}) custom-call(f32[8,128]{1,0:T(8,128)} %get-tuple-element.14.gains_ref, bf16[512,1024]{1,0:T(8,128)(2,1)} %get-tuple-element.15.gq_ref, bf16[512,128]{1,0:T(8,128)(2,1)} %get-tuple-element.16.gk_ref, ...), custom_call_target="tpu_custom_call" | custom-call | tf_op jit(solution)/shard_map/pallas_call | solution.py:780

commit v4 on v3

--- a/solution.py
+++ b/solution.py
@@ -14,6 +14,8 @@
 POS = 27
 RT = 1024
 CBP = 8
+MG = 64
+NG = BLK // MG
 CBL = 10
 HT = RT // BLK
 CS = 256
@@ -91,7 +93,7 @@
     other = 2 * (1 - y) + c
 
     def krows(g, h):
-        return kv_ref.at[pl.ds(pl.multiple_of(g * GRP + h * 256, 256), 256)]
+        return kv_ref.at[pl.ds(pl.multiple_of(g * GRP + h * BLK, BLK), BLK)]
 
     def kblocks(first, count):
         return kv_ref.at[pl.ds(first * BLK, count * BLK)]
@@ -104,7 +106,7 @@
 
     def kv_s(j, h):
         g = chain if j == 0 else other
-        return copy_to(krows(g, h), krows(g, h), send_s.at[2 * j + h], recv_s.at[2 * j + h], dp, sib)
+        return copy_to(krows(g, h), krows(g, h), send_s.at[4 * j + h], recv_s.at[4 * j + h], dp, sib)
 
     has_next = (n >= 2) & (n + 1 <= 7)
     has_prev = n >= 3
@@ -116,15 +118,17 @@
     sends_kfar = (c == 1) & (n >= 2) & (n + 2 <= 7)
     gets_kfar = (c == 0) & (n >= 4)
 
+    shift = jnp.where(z >= 2, 2, 0)
+    pieces = [lax.rem(p + shift, 4) for p in range(4)]
+
     @pl.when(z == 0)
     def _():
-        kv_z(0, 1, 0).start()
-        kv_z(1, 3, 1).start()
-        kv_z(1, 1, 2).start()
-        kv_z(0, 3, 3).start()
-        for h in (0, 1):
-            kv_y(h).start()
-            kv_s(0, h).start()
+        for p in range(4):
+            kv_z(p, 1, 2 * p).start()
+            kv_z((p + 2) % 4, 3, 2 * p + 1).start()
+        for p in range(4):
+            kv_y(p).start()
+            kv_s(0, p).start()
 
     @pl.when((c == 0) & (n >= 2))
     def _():
@@ -344,31 +348,17 @@
         return 0
 
     lax.fori_loop(0, 2, prep, 0)
-    def got(h):
-        kv_z(h, 0, 0).wait_recv()
-        kv_y(h).start()
-        kv_s(0, h).start()
-
-    @pl.when(z == 1)
-    def _():
-        kv_z(0, 2, 0).wait_recv()
-        kv_z(0, 2, 0).start()
-        kv_y(0).start()
-        kv_s(0, 0).start()
-        got(1)
-
-    @pl.when(z == 3)
-    def _():
-        kv_z(1, 2, 0).wait_recv()
-        kv_z(1, 2, 0).start()
-        kv_y(1).start()
-        kv_s(0, 1).start()
-        got(0)
-
-    @pl.when(z == 2)
-    def _():
-        got(0)
-        got(1)
+    @pl.when(z != 0)
+    def _():
+        for p in range(4):
+            h = pieces[p]
+            kv_z(h, 0, 0).wait_recv()
+            if p < 2:
+                @pl.when(z != 2)
+                def _():
+                    kv_z(h, 2, p).start()
+            kv_y(h).start()
+            kv_s(0, h).start()
 
     lax.fori_loop(2, 4, prep, 0)
     @pl.when(has_prev)
@@ -383,30 +373,24 @@
     def _():
         relay_half.start()
 
-    def y_got(h):
-        copy_to(krows(other, h), krows(other, h), send_y.at[h], recv_y.at[h], dp, yny).wait_recv()
-        kv_s(1, h).start()
-
-    @pl.when(z != 3)
-    def _():
-        y_got(0)
-        y_got(1)
-
-    @pl.when(z == 3)
-    def _():
-        y_got(1)
-        y_got(0)
-
-    for j in (0, 1):
-        for h in (0, 1):
-            g = (2 * y + 1 - c) if j == 0 else (2 * (1 - y) + 1 - c)
-            copy_to(krows(g, h), krows(g, h), send_s.at[2 * j + h], recv_s.at[2 * j + h], dp, sib).wait_recv()
+    def chain_arrive():
+        g = 2 * y + 1 - c
+        for h in pieces:
+            copy_to(krows(g, h), krows(g, h), send_s.at[h], recv_s.at[h], dp, sib).wait_recv()
+
+    def rest_arrive():
+        for h in pieces:
+            copy_to(krows(other, h), krows(other, h), send_y.at[h], recv_y.at[h], dp, yny).wait_recv()
+            kv_s(1, h).start()
+        g = 2 * (1 - y) + 1 - c
+        for h in pieces:
+            copy_to(krows(g, h), krows(g, h), send_s.at[4 + h], recv_s.at[4 + h], dp, sib).wait_recv()
+        lax.fori_loop(0, PROMPT, slot_t, 0)
 
     def slot_t(s, _):
         kt[s] = kv_ref[pl.ds(pl.multiple_of(s * BLK, BLK), BLK), 0:BLK].T
         return 0
 
-    lax.fori_loop(0, PROMPT, slot_t, 0)
     lax.fori_loop(OWN, SLOTS, slot_t, 0)
 
     def local_arrive():
@@ -426,6 +410,7 @@
         n_prev = jnp.clip(b - PROMPT, 0, REACH)
         pc = (n_prompt + CBP - 1) // CBP
         lc = (REACH - n_prev) // CBL
+        whole = jnp.minimum(n_prompt, 1)
         keyi = lax.broadcasted_iota(jnp.int32, (BLK, RT), 0)
         toki = lax.rem(lax.broadcasted_iota(jnp.int32, (BLK, RT), 1), BLK)
         bias = jnp.where((keyi <= toki) & (keyi < live), 0.0, LOW)
@@ -450,36 +435,45 @@
                     cs = slice(x, x + CS)
                     s = nn(kc, qt[t, :, cs])
                     for u in range(nb):
-                        su = s[u * BLK:(u + 1) * BLK]
-                        if diag:
-                            su = su + bias[:, cs]
-                        su = su.reshape(BLK // 8, 8, CS)
-                        m = jnp.max(su, axis=0) * SL2
-                        w = jnp.exp2(su * SL2 - m[None])
-                        s_s[pos + u, :, cs] = jnp.sum(w, axis=0)
-                        if diag:
-                            m_s[pos + u, :, cs] = m
-                        else:
-                            m_s[pos + u, :, cs] = jnp.where(seen(pos + u), m, LOW)
-                        w_s[pos + u, :, cs] = w.reshape(BLK, CS)
-
-            def over(body, init, between=None):
-                init = lax.fori_loop(0, pc, lambda c, x: body(c * CBP, CBP, False, x), init)
-                if between is not None:
-                    between()
+                        for q in range(NG):
+                            lo = u * BLK + q * MG
+                            su = s[lo:lo + MG]
+                            if diag:
+                                su = su + bias[q * MG:(q + 1) * MG, cs]
+                            su = su.reshape(MG // 8, 8, CS)
+                            m = jnp.max(su, axis=0) * SL2
+                            w = jnp.exp2(su * SL2 - m[None])
+                            s_s[(pos + u) * NG + q, :, cs] = jnp.sum(w, axis=0)
+                            if diag:
+                                m_s[(pos + u) * NG + q, :, cs] = m
+                            else:
+                                m_s[(pos + u) * NG + q, :, cs] = jnp.where(seen(pos + u), m, LOW)
+                            w_s[pos + u, q * MG:(q + 1) * MG, cs] = w.reshape(MG, CS)
+
+            def local(body, init):
                 init = lax.fori_loop(lc, REACH // CBL, lambda c, x: body(PROMPT + c * CBL, CBL, False, x), init)
                 return body(POS - 1, 1, True, init)
+
+            def over(body, init):
+                return local(body, lax.fori_loop(0, whole, lambda c, x: body(0, PROMPT, False, x), init))
 
             def p1(pos, nb, diag, x):
                 first_pass(pos, nb, diag)
                 return x
 
-            def await_local():
-                @pl.when(i == 0)
-                def _():
-                    local_arrive()
-
-            over(p1, 0, await_local)
+            @pl.when(i == 0)
+            def _():
+                local_arrive()
+                local(p1, 0)
+                chain_arrive()
+                lax.fori_loop(0, whole, lambda c, x: p1(y * CBP, CBP, False, x), 0)
+                rest_arrive()
+                lax.fori_loop(0, whole, lambda c, x: p1((1 - y) * CBP, CBP, False, x), 0)
+
+            @pl.when(i > 0)
+            def _():
+                over(p1, 0)
+
             m = m_s[...]
             top = jnp.max(jnp.max(m, axis=0), axis=0, keepdims=True)
             f = jnp.exp2(m - top[None])
@@ -498,7 +492,11 @@
                     pu = []
                     for u in range(nb):
                         du = dp[u * BLK:(u + 1) * BLK]
-                        ch = (w_s[pos + u, :, cs].reshape(BLK // 8, 8, CS) * f_s[pos + u, :, cs][None]).reshape(BLK, CS)
+                        parts = []
+                        for q in range(NG):
+                            wq = w_s[pos + u, q * MG:(q + 1) * MG, cs].reshape(MG // 8, 8, CS)
+                            parts.append((wq * f_s[(pos + u) * NG + q, :, cs][None]).reshape(MG, CS))
+                        ch = jnp.concatenate(parts, axis=0)
                         chb = ch.astype(BF)
                         w_s[pos + u, :, cs] = ch
                         dp_s[pos + u, :, cs] = du
@@ -533,10 +531,10 @@
                 dk_ref[rows, :] += nn(ds, qrows)
                 slot = r0 // BLK
                 ktc = jnp.concatenate([kt[slot + u] for u in range(nb)], axis=1) if nb > 1 else kt[slot]
-                dq_s[...] += nn(ktc, ds)
+                dq_s[i] += nn(ktc, ds)
                 return 0
 
-            dq_s[...] = jnp.zeros_like(dq_s)
+            dq_s[i] = jnp.zeros((BLK, RT), F32)
             p4(POS - 1, 1, True, 0)
             lax.fori_loop(lc, REACH // CBL, lambda c, x: p4(PROMPT + c * CBL, CBL, False, x), 0)
 
@@ -567,27 +565,33 @@
                 cp_a(1, 1).start()
                 stage_d(0)
 
-            dqt = dq_s[...]
-            dq = dqt.T * SCALE
-            rows = pl.ds(pl.multiple_of(i * BLK, BLK), BLK)
-            part = jnp.zeros((8, BLK), F32)
-            for u in range(HT):
-                cols = pl.ds(pl.multiple_of((g * HT + u) * BLK, BLK), BLK)
-                x = q_ref[rows, cols].astype(F32)
-                r = lax.rsqrt(jnp.mean(x * x, axis=-1, keepdims=True) + 1e-6)
-                unit = x * r
-                dqu = dq[u * BLK:(u + 1) * BLK]
-                both = dqu * unit
-                part = part + jnp.sum(both.reshape(BLK // 8, 8, BLK), axis=0)
-                mean = jnp.mean(both * gain, axis=-1, keepdims=True)
-                gq_ref[rows, cols] = (r * (dqu * gain - unit * mean)).astype(BF)
-            qpart[...] += part
             return 0
 
         lax.fori_loop(0, TPB, per_tile, 0)
         return 0
 
     lax.fori_loop(0, 4, per_block, 0)
+    stage_b(1)
+
+    def finish(i, _):
+        dqt = dq_s[i]
+        dq = dqt.T * SCALE
+        rows = pl.ds(pl.multiple_of(i * BLK, BLK), BLK)
+        part = jnp.zeros((8, BLK), F32)
+        for u in range(HT):
+            cols = pl.ds(pl.multiple_of(u * BLK, BLK), BLK)
+            x = q_ref[rows, cols].astype(F32)
+            r = lax.rsqrt(jnp.mean(x * x, axis=-1, keepdims=True) + 1e-6)
+            unit = x * r
+            dqu = dq[u * BLK:(u + 1) * BLK]
+            both = dqu * unit
+            part = part + jnp.sum(both.reshape(BLK // 8, 8, BLK), axis=0)
+            mean = jnp.mean(both * gain, axis=-1, keepdims=True)
+            gq_ref[rows, cols] = (r * (dqu * gain - unit * mean)).astype(BF)
+        qpart[...] += part
+        return 0
+
+    lax.fori_loop(0, 4, finish, 0)
 
     def key_part(k, acc):
         rr = pl.ds(pl.multiple_of(k * BLK, BLK), BLK)
@@ -604,7 +608,6 @@
     for q in cg:
         q.start()
     gall[me] = gown[...]
-    stage_b(1)
     stage_e(0)
     for h in (0, 1):
         cp_b(1, h).wait_send()
@@ -673,14 +676,15 @@
 
     @pl.when(z == 0)
     def _():
-        for k in range(4):
+        for k in range(8):
             kv_z(0, 1, k).wait_send()
 
     @pl.when((z == 1) | (z == 3))
     def _():
-        kv_z(0, 1, 0).wait_send()
-
-    for h in (0, 1):
+        for k in range(2):
+            kv_z(0, 1, k).wait_send()
+
+    for h in range(4):
         kv_y(h).wait_send()
         kv_s(0, h).wait_send()
         kv_s(1, h).wait_send()
@@ -731,10 +735,10 @@
             pltpu.VMEM((SLOTS, BLK, BLK), BF),
             pltpu.VMEM((POS, BLK, RT), F32),
             pltpu.VMEM((POS, BLK, RT), F32),
-            pltpu.VMEM((POS, 8, RT), F32),
-            pltpu.VMEM((POS, 8, RT), F32),
-            pltpu.VMEM((POS, 8, RT), F32),
-            pltpu.VMEM((BLK, RT), F32),
+            pltpu.VMEM((POS * NG, 8, RT), F32),
+            pltpu.VMEM((POS * NG, 8, RT), F32),
+            pltpu.VMEM((POS * NG, 8, RT), F32),
+            pltpu.VMEM((tiles, BLK, RT), F32),
             pltpu.VMEM((rows, BLK), F32),
             pltpu.VMEM((rows, BLK), F32),
             pltpu.VMEM((8, BLK), F32),
@@ -745,7 +749,7 @@
             pltpu.VMEM((8, BLK), F32),
             pltpu.VMEM((16, 8, BLK), F32),
             pltpu.VMEM((8, 8, BLK), F32),
-        ] + [dma((m,)) for m in (4, 2, 2, 2, 4, 4, 5, 3, 4, 4, 4, 4, 4, 8, 8, 8, 22, 24)],
+        ] + [dma((m,)) for m in (8, 4, 4, 4, 8, 8, 5, 3, 4, 4, 4, 4, 4, 8, 8, 8, 22, 24)],
         compiler_params=pltpu.CompilerParams(
             collective_id=0, has_side_effects=True, vmem_limit_bytes=60 * 1024 * 1024),
     )(lens, frm, qg, kg, q, do, k, v)

time: 109 us -> 102 us (0.936)
  Pallas kernels: 108 us -> 102 us
    pallas_call x1, Pallas kernels: 105 us -> 98.4 us  [fused(): pl.pallas_call(fused_kernel, out_shape=(jax.ShapeDtypeStruct((512, 1024),...]
where the time goes in v4:
time: 102 us
  Pallas kernels  102 us (100%)
    pallas_call x1, Pallas kernels, fused(): pl.pallas_call(fused_kernel, out_shape=(jax.ShapeDtypeStruct((512, 1024),...  98.4 us
    pallas_call x1, Pallas kernels, hand_out(): pl.pallas_call(hand_out_kernel, out_shape=tuple((jax.ShapeDtypeStruct(t.s...  3.29 us

profile of v4, /device:TPU:1, one launch (start us, length us, event | category | flops | bytes accessed | tf_op | source)
XLA Modules:
  0.0 102.3 jit_solution(7515451690921404766)
XLA Ops:
  0.6 98.4 %shard_map.119 = (bf16[512,1024]{1,0:T(8,128)(2,1)}, bf16[512,128]{1,0:T(8,128)(2,1)}, bf16[512,128]{1,0:T(8,128)(2,1)}, f32[8,128]{1,0:T(8,128)}) custom-call(s32[8]{0:T(128)} %bitcast.15, s32[4]{0:T(128)} %bitcast.16, f32[1,128]{1,0:T(1,128)} %bitcast.17, f32[1,128]{1,0:T(1,128)} %bitcast.18, bf16[512,1024]{1,0:T(8,128)(2,1)} %bitcast.11, ...), custom_call_target="tpu_custom_call" | custom-call | tf_op jit(solution)/shard_map/pallas_call | solution.py:719
  99.0 3.3 %shard_map.120 = (bf16[512,1024]{1,0:T(8,128)(2,1)}, bf16[512,128]{1,0:T(8,128)(2,1)}, bf16[512,128]{1,0:T(8,128)(2,1)}, f32[128]{0:T(128)}, f32[128]{0:T(128)}) custom-call(f32[8,128]{1,0:T(8,128)} %get-tuple-element.14.gains_ref, bf16[512,1024]{1,0:T(8,128)(2,1)} %get-tuple-element.15.gq_ref, bf16[512,128]{1,0:T(8,128)(2,1)} %get-tuple-element.16.gk_ref, ...), custom_call_target="tpu_custom_call" | custom-call | tf_op jit(solution)/shard_map/pallas_call | solution.py:784

commit v5 on v4

--- a/solution.py
+++ b/solution.py
@@ -48,24 +48,17 @@
         device_id=(dp, ctx), device_id_type=MESH)
 
 
-def greet(dp, me, wide):
+def announce(dp, me):
     barrier = pltpu.get_barrier_semaphore()
-    c = lax.rem(me, 2)
-    y = lax.rem(me // 2, 2)
-    if wide:
-        targets = [(dp, lax.rem(me + o, 16)) for o in range(1, 16)]
-        targets += [(lax.rem(dp + o, 8), me) for o in range(1, 8)]
-    else:
-        targets = [(dp, me + 1 - 2 * c), (dp, me + 2 - 4 * y)]
-        targets += [(dp, lax.rem(me + o, 16)) for o in (4, 12, 2, 14, 3, 13)]
+    targets = [(dp, lax.rem(me + o, 16)) for o in range(1, 16)]
+    targets += [(lax.rem(dp + o, 8), me) for o in range(1, 8)]
     for t in targets:
         pl.semaphore_signal(barrier, inc=1, device_id=t, device_id_type=MESH)
-    pl.semaphore_wait(barrier, len(targets))
-
-
-def fused_kernel(len_ref, from_ref, qg_ref, kg_ref, q_ref, do_ref, k_ref, v_ref,
-                 gq_ref, gk_ref, gv_ref, gain_ref,
-                 kv_ref, qn, qt, dn, dt, kt, w_s, dp_s, m_s, s_s, f_s, dq_s, dk_ref, dv_ref, qpart,
+
+
+def fused_kernel(len_ref, from_ref, qg_ref, kg_ref, q_in, do_in, k_in, v_in,
+                 gq_out, gk_ref, gv_ref, gain_ref,
+                 q_ref, do_ref, k_ref, v_ref, gq_ref, in_sem, out_sem, kv_ref, qn, qt, dn, dt, kt, w_s, dp_s, m_s, s_s, f_s, dq_s, dk_ref, dv_ref, qpart,
                  away, bufa, bufb, bufc, bufl, bufs, sa, sb, sl, tot, gown, gsum, gall, gdp,
                  send_z, recv_z, send_y, recv_y, send_s, recv_s, fsend_l, frecv_l,
                  send_a, recv_a, send_b, recv_b, send_c, recv_c, send_l, recv_l, send_g, recv_g):
@@ -78,7 +71,14 @@
     first = me * 4
     sib = me + 1 - 2 * c
     yny = me + 2 - 4 * y
+    arriving = [pltpu.make_async_copy(src, dst, in_sem.at[j])
+                for j, (src, dst) in enumerate(((k_in, k_ref), (v_in, v_ref), (q_in, q_ref), (do_in, do_ref)))]
+    for copy in arriving:
+        copy.start()
     kv_ref[PROMPT * BLK:OWN * BLK, :] = jnp.zeros((REACH * BLK, 2 * BLK), BF)
+    announce(dp, me)
+    arriving[0].wait()
+    arriving[1].wait()
     x = k_ref[...].astype(F32)
     r = lax.rsqrt(jnp.mean(x * x, axis=-1, keepdims=True) + 1e-6)
     kv_ref[OWN * BLK:, 0:BLK] = (x * r * kg_ref[...]).astype(BF)
@@ -88,7 +88,7 @@
     def _():
         kv_ref[pl.ds(pl.multiple_of(me * GRP, GRP), GRP), :] = kv_ref[OWN * BLK:, :]
 
-    greet(dp, me, True)
+    pl.semaphore_wait(pltpu.get_barrier_semaphore(), 22)
     chain = 2 * y + c
     other = 2 * (1 - y) + c
 
@@ -347,6 +347,8 @@
             dt[t, :, e] = z.T
         return 0
 
+    arriving[2].wait()
+    arriving[3].wait()
     lax.fori_loop(0, 2, prep, 0)
     @pl.when(z != 0)
     def _():
@@ -520,50 +522,59 @@
             delta = jnp.sum(delta, axis=0, keepdims=True)
             qrows = qn[t]
 
-            def p4(pos, nb, diag, dq):
-                r0 = row0(pos)
+            def key_side(pos, nb, keep):
+                rr = pl.ds(row0(pos), nb * BLK)
                 dss = []
                 for u in range(nb):
-                    ch = w_s[pos + u]
-                    dss.append((ch * (dp_s[pos + u] - delta)).astype(BF))
+                    ds = (w_s[pos + u] * (dp_s[pos + u] - delta)).astype(BF)
+                    if keep:
+                        w_s[pos + u] = ds.astype(F32)
+                    dss.append(ds)
                 ds = jnp.concatenate(dss, axis=0) if nb > 1 else dss[0]
-                rows = pl.ds(r0, nb * BLK)
-                dk_ref[rows, :] += nn(ds, qrows)
-                slot = r0 // BLK
+                dk_ref[rr, :] += nn(ds, qrows)
+                return ds
+
+            def query_side(pos, nb, ds):
+                slot = row0(pos) // BLK
                 ktc = jnp.concatenate([kt[slot + u] for u in range(nb)], axis=1) if nb > 1 else kt[slot]
                 dq_s[i] += nn(ktc, ds)
-                return 0
+
+            def p4(pos, nb, diag, dq):
+                query_side(pos, nb, key_side(pos, nb, False))
+                return dq
+
+            def p4_keys(pos, nb, diag, dq):
+                key_side(pos, nb, True)
+                return dq
+
+            def p4_queries(pos, nb, diag, dq):
+                parts = [w_s[pos + u].astype(BF) for u in range(nb)]
+                query_side(pos, nb, jnp.concatenate(parts, axis=0) if nb > 1 else parts[0])
+                return dq
 
             dq_s[i] = jnp.zeros((BLK, RT), F32)
-            p4(POS - 1, 1, True, 0)
-            lax.fori_loop(lc, REACH // CBL, lambda c, x: p4(PROMPT + c * CBL, CBL, False, x), 0)
+
+            @pl.when(i < 3)
+            def _():
+                lax.fori_loop(0, pc, lambda c, x: p4(c * CBP, CBP, False, x), 0)
+                local(p4, 0)
 
             @pl.when(i == 3)
             def _():
+                for j in (0, 1):
+                    @pl.when(j < pc)
+                    def _(j=j):
+                        p4_keys(j * CBP, CBP, False, 0)
+
+                    hand_over(1, 8 * j, 8 * j + 8)
+                    cp_a(1, j).start()
+                stage_b(0)
+                local(p4_keys, 0)
                 hand_over(1, PROMPT, OWN)
+                stage_b(1)
                 local_start(1)
-                stage_b(0)
-                local_mid(0)
-
-            @pl.when(0 < pc)
-            def _():
-                p4(0, CBP, False, 0)
-
-            @pl.when(i == 3)
-            def _():
-                hand_over(1, 0, 8)
-                cp_a(1, 0).start()
-                stage_c(0)
-
-            @pl.when(1 < pc)
-            def _():
-                p4(CBP, CBP, False, 0)
-
-            @pl.when(i == 3)
-            def _():
-                hand_over(1, 8, PROMPT)
-                cp_a(1, 1).start()
-                stage_d(0)
+                lax.fori_loop(0, pc, lambda c, x: p4_queries(c * CBP, CBP, False, x), 0)
+                local(p4_queries, 0)
 
             return 0
 
@@ -571,7 +582,6 @@
         return 0
 
     lax.fori_loop(0, 4, per_block, 0)
-    stage_b(1)
 
     def finish(i, _):
         dqt = dq_s[i]
@@ -592,6 +602,8 @@
         return 0
 
     lax.fori_loop(0, 4, finish, 0)
+    leaving = pltpu.make_async_copy(gq_ref, gq_out, out_sem.at[0])
+    leaving.start()
 
     def key_part(k, acc):
         rr = pl.ds(pl.multiple_of(k * BLK, BLK), BLK)
@@ -608,10 +620,11 @@
     for q in cg:
         q.start()
     gall[me] = gown[...]
-    stage_e(0)
-    for h in (0, 1):
-        cp_b(1, h).wait_send()
-    local_mid(1)
+    for x in (0, 1):
+        for h in (0, 1):
+            cp_b(x, h).wait_send()
+        local_mid(x)
+    stage_c(0)
     stage_c(1)
     for o in range(1, 16):
         p = lax.rem(me + o, 16)
@@ -623,9 +636,11 @@
     for q in ch:
         q.start()
     gdp[dp] = total
+    stage_d(0)
+    stage_d(1)
+    stage_e(0)
     local_end(0)
     gv_ref[...] = tot[0].astype(BF)
-    stage_d(1)
     stage_e(1)
     local_end(1)
     x = k_ref[...].astype(F32)
@@ -643,11 +658,10 @@
     gain_ref[...] = total
     for q in cg + ch:
         q.wait_send()
+    leaving.wait()
     for x in (0, 1):
         for h in (0, 1):
             cp_a(x, h).wait_send()
-            if x == 0:
-                cp_b(x, h).wait_send()
 
         @pl.when(z != 0)
         def _(x=x):
@@ -715,6 +729,8 @@
     rows = SLOTS * BLK
     tiles = 4096 // RT
     pair = pltpu.VMEM((2, GRP, BLK), BF)
+    anywhere = pl.BlockSpec(memory_space=pl.ANY)
+    wide, narrow = pltpu.VMEM((GRP, 8 * BLK), BF), pltpu.VMEM((GRP, BLK), BF)
     two = pltpu.VMEM((2, 2, GRP, BLK), BF)
     return pl.pallas_call(
         fused_kernel,
@@ -724,9 +740,10 @@
             jax.ShapeDtypeStruct((GRP, BLK), BF),
             jax.ShapeDtypeStruct((8, BLK), F32),
         ),
-        in_specs=[SM, SM, VM, VM, VM, VM, VM, VM],
-        out_specs=(VM, VM, VM, VM),
+        in_specs=[SM, SM, VM, VM] + [anywhere] * 4,
+        out_specs=(anywhere, VM, VM, VM),
         scratch_shapes=[
+            wide, wide, narrow, narrow, wide, dma((4,)), dma((1,)),
             pltpu.VMEM((rows, 2 * BLK), BF),
             pltpu.VMEM((tiles, RT, BLK), BF),
             pltpu.VMEM((tiles, BLK, RT), BF),

time: 102 us -> 95.8 us (0.939)
  Pallas kernels: 102 us -> 94.8 us
    pallas_call x1, Pallas kernels: 98.4 us -> 91.5 us  [fused(): pl.pallas_call(fused_kernel, out_shape=(jax.ShapeDtypeStruct((512, 1024),...]
where the time goes in v5:
time: 95.8 us; the launch traced here: 95.4 us
  Pallas kernels  94.8 us (99%)
    pallas_call x1, Pallas kernels, fused(): pl.pallas_call(fused_kernel, out_shape=(jax.ShapeDtypeStruct((512, 1024),...  91.5 us
    pallas_call x1, Pallas kernels, hand_out(): pl.pallas_call(hand_out_kernel, out_shape=tuple((jax.ShapeDtypeStruct(t.s...  3.29 us

profile of v5, /device:TPU:1, one launch (start us, length us, event | category | flops | bytes accessed | tf_op | source)
XLA Modules:
  0.0 95.4 jit_solution(10949775302573762375)
XLA Ops:
  0.6 91.5 %shard_map.119 = (bf16[512,1024]{1,0:T(8,128)(2,1)}, bf16[512,128]{1,0:T(8,128)(2,1)}, bf16[512,128]{1,0:T(8,128)(2,1)}, f32[8,128]{1,0:T(8,128)}) custom-call(s32[8]{0:T(128)} %bitcast.15, s32[4]{0:T(128)} %bitcast.16, f32[1,128]{1,0:T(1,128)} %bitcast.17, f32[1,128]{1,0:T(1,128)} %bitcast.18, bf16[512,1024]{1,0:T(8,128)(2,1)} %bitcast.11, ...), custom_call_target="tpu_custom_call" | custom-call | tf_op jit(solution)/shard_map/pallas_call | solution.py:735
  92.1 3.3 %shard_map.120 = (bf16[512,1024]{1,0:T(8,128)(2,1)}, bf16[512,128]{1,0:T(8,128)(2,1)}, bf16[512,128]{1,0:T(8,128)(2,1)}, f32[128]{0:T(128)}, f32[128]{0:T(128)}) custom-call(f32[8,128]{1,0:T(8,128)} %get-tuple-element.14.gains_ref, bf16[512,1024]{1,0:T(8,128)(2,1)} %get-tuple-element.15.gq_ref, bf16[512,128]{1,0:T(8,128)(2,1)} %get-tuple-element.16.gk_ref, ...), custom_call_target="tpu_custom_call" | custom-call | tf_op jit(solution)/shard_map/pallas_call | solution.py:801

commit v6 on v5

--- a/solution.py
+++ b/solution.py
@@ -16,7 +16,6 @@
 CBP = 8
 MG = 64
 NG = BLK // MG
-CBL = 10
 HT = RT // BLK
 CS = 256
 TPB = HEADS // HT
@@ -58,7 +57,7 @@
 
 def fused_kernel(len_ref, from_ref, qg_ref, kg_ref, q_in, do_in, k_in, v_in,
                  gq_out, gk_ref, gv_ref, gain_ref,
-                 q_ref, do_ref, k_ref, v_ref, gq_ref, in_sem, out_sem, kv_ref, qn, qt, dn, dt, kt, w_s, dp_s, m_s, s_s, f_s, dq_s, dk_ref, dv_ref, qpart,
+                 q_ref, do_ref, k_ref, v_ref, gq_ref, in_sem, out_sem, kv_ref, qn, qt, dn, dt, kt, w_s, dp_s, m_s, s_s, dq_s, dk_ref, dv_ref, qpart,
                  away, bufa, bufb, bufc, bufl, bufs, sa, sb, sl, tot, gown, gsum, gall, gdp,
                  send_z, recv_z, send_y, recv_y, send_s, recv_s, fsend_l, frecv_l,
                  send_a, recv_a, send_b, recv_b, send_c, recv_c, send_l, recv_l, send_g, recv_g):
@@ -409,9 +408,7 @@
     def per_block(i, _):
         b, off, live = facts(i)
         n_prompt = jnp.minimum(b, PROMPT)
-        n_prev = jnp.clip(b - PROMPT, 0, REACH)
         pc = (n_prompt + CBP - 1) // CBP
-        lc = (REACH - n_prev) // CBL
         whole = jnp.minimum(n_prompt, 1)
         keyi = lax.broadcasted_iota(jnp.int32, (BLK, RT), 0)
         toki = lax.rem(lax.broadcasted_iota(jnp.int32, (BLK, RT), 1), BLK)
@@ -440,21 +437,21 @@
                         for q in range(NG):
                             lo = u * BLK + q * MG
                             su = s[lo:lo + MG]
-                            if diag:
+                            own = diag and u == nb - 1
+                            if own:
                                 su = su + bias[q * MG:(q + 1) * MG, cs]
                             su = su.reshape(MG // 8, 8, CS)
                             m = jnp.max(su, axis=0) * SL2
                             w = jnp.exp2(su * SL2 - m[None])
                             s_s[(pos + u) * NG + q, :, cs] = jnp.sum(w, axis=0)
-                            if diag:
+                            if own:
                                 m_s[(pos + u) * NG + q, :, cs] = m
                             else:
                                 m_s[(pos + u) * NG + q, :, cs] = jnp.where(seen(pos + u), m, LOW)
                             w_s[pos + u, q * MG:(q + 1) * MG, cs] = w.reshape(MG, CS)
 
             def local(body, init):
-                init = lax.fori_loop(lc, REACH // CBL, lambda c, x: body(PROMPT + c * CBL, CBL, False, x), init)
-                return body(POS - 1, 1, True, init)
+                return body(PROMPT, REACH + 1, True, init)
 
             def over(body, init):
                 return local(body, lax.fori_loop(0, whole, lambda c, x: body(0, PROMPT, False, x), init))
@@ -480,7 +477,7 @@
             top = jnp.max(jnp.max(m, axis=0), axis=0, keepdims=True)
             f = jnp.exp2(m - top[None])
             tot = jnp.sum(jnp.sum(f * s_s[...], axis=0), axis=0, keepdims=True)
-            f_s[...] = f * (1.0 / tot)[None]
+            m_s[...] = f * (1.0 / tot)[None]
 
             drows = dn[t]
             def p3(pos, nb, diag, acc):
@@ -497,7 +494,7 @@
                         parts = []
                         for q in range(NG):
                             wq = w_s[pos + u, q * MG:(q + 1) * MG, cs].reshape(MG // 8, 8, CS)
-                            parts.append((wq * f_s[(pos + u) * NG + q, :, cs][None]).reshape(MG, CS))
+                            parts.append((wq * m_s[(pos + u) * NG + q, :, cs][None]).reshape(MG, CS))
                         ch = jnp.concatenate(parts, axis=0)
                         chb = ch.astype(BF)
                         w_s[pos + u, :, cs] = ch
@@ -754,7 +751,6 @@
             pltpu.VMEM((POS, BLK, RT), F32),
             pltpu.VMEM((POS * NG, 8, RT), F32),
             pltpu.VMEM((POS * NG, 8, RT), F32),
-            pltpu.VMEM((POS * NG, 8, RT), F32),
             pltpu.VMEM((tiles, BLK, RT), F32),
             pltpu.VMEM((rows, BLK), F32),
             pltpu.VMEM((rows, BLK), F32),
@@ -768,7 +764,7 @@
             pltpu.VMEM((8, 8, BLK), F32),
         ] + [dma((m,)) for m in (8, 4, 4, 4, 8, 8, 5, 3, 4, 4, 4, 4, 4, 8, 8, 8, 22, 24)],
         compiler_params=pltpu.CompilerParams(
-            collective_id=0, has_side_effects=True, vmem_limit_bytes=60 * 1024 * 1024),
+            collective_id=0, has_side_effects=True, vmem_limit_bytes=62 * 1024 * 1024),
     )(lens, frm, qg, kg, q, do, k, v)
 
 

time: 95.8 us -> 93.8 us (0.979)
  Pallas kernels: 94.8 us -> 92.9 us
    pallas_call x1, Pallas kernels: 91.5 us -> 89.6 us  [fused(): pl.pallas_call(fused_kernel, out_shape=(jax.ShapeDtypeStruct((512, 1024),...]
where the time goes in v6:
time: 93.8 us; the launch traced here: 93.5 us
  Pallas kernels  92.9 us (99%)
    pallas_call x1, Pallas kernels, fused(): pl.pallas_call(fused_kernel, out_shape=(jax.ShapeDtypeStruct((512, 1024),...  89.6 us
    pallas_call x1, Pallas kernels, hand_out(): pl.pallas_call(hand_out_kernel, out_shape=tuple((jax.ShapeDtypeStruct(t.s...  3.29 us

profile of v6, /device:TPU:1, one launch (start us, length us, event | category | flops | bytes accessed | tf_op | source)
XLA Modules:
  0.0 93.5 jit_solution(17802717177361654149)
XLA Ops:
  0.6 89.6 %shard_map.119 = (bf16[512,1024]{1,0:T(8,128)(2,1)}, bf16[512,128]{1,0:T(8,128)(2,1)}, bf16[512,128]{1,0:T(8,128)(2,1)}, f32[8,128]{1,0:T(8,128)}) custom-call(s32[8]{0:T(128)} %bitcast.15, s32[4]{0:T(128)} %bitcast.16, f32[1,128]{1,0:T(1,128)} %bitcast.17, f32[1,128]{1,0:T(1,128)} %bitcast.18, bf16[512,1024]{1,0:T(8,128)(2,1)} %bitcast.11, ...), custom_call_target="tpu_custom_call" | custom-call | tf_op jit(solution)/shard_map/pallas_call | solution.py:732
  90.2 3.3 %shard_map.120 = (bf16[512,1024]{1,0:T(8,128)(2,1)}, bf16[512,128]{1,0:T(8,128)(2,1)}, bf16[512,128]{1,0:T(8,128)(2,1)}, f32[128]{0:T(128)}, f32[128]{0:T(128)}) custom-call(f32[8,128]{1,0:T(8,128)} %get-tuple-element.14.gains_ref, bf16[512,1024]{1,0:T(8,128)(2,1)} %get-tuple-element.15.gq_ref, bf16[512,128]{1,0:T(8,128)(2,1)} %get-tuple-element.16.gk_ref, ...), custom_call_target="tpu_custom_call" | custom-call | tf_op jit(solution)/shard_map/pallas_call | solution.py:797

commit v7 on v6

--- a/solution.py
+++ b/solution.py
@@ -57,7 +57,7 @@
 
 def fused_kernel(len_ref, from_ref, qg_ref, kg_ref, q_in, do_in, k_in, v_in,
                  gq_out, gk_ref, gv_ref, gain_ref,
-                 q_ref, do_ref, k_ref, v_ref, gq_ref, in_sem, out_sem, kv_ref, qn, qt, dn, dt, kt, w_s, dp_s, m_s, s_s, dq_s, dk_ref, dv_ref, qpart,
+                 q_ref, do_ref, k_ref, v_ref, gq_ref, in_sem, out_sem, kv_ref, qn, qt, dn, dt, kt, w_s, dp_s, m_s, s_s, dl_s, dq_s, dk_ref, dv_ref, qpart,
                  away, bufa, bufb, bufc, bufl, bufs, sa, sb, sl, tot, gown, gsum, gall, gdp,
                  send_z, recv_z, send_y, recv_y, send_s, recv_s, fsend_l, frecv_l,
                  send_a, recv_a, send_b, recv_b, send_c, recv_c, send_l, recv_l, send_g, recv_g):
@@ -427,12 +427,15 @@
             def row0(pos):
                 return pl.multiple_of(jnp.where(pos < PROMPT, pos, pos + i) * BLK, BLK)
 
-            def first_pass(pos, nb, diag):
+            def first_pass(pos, nb, diag, ahead_dp):
                 r0 = row0(pos)
                 kc = kv_ref[pl.ds(r0, nb * BLK), 0:BLK]
+                vc = kv_ref[pl.ds(r0, nb * BLK), BLK:2 * BLK]
                 for x in range(0, RT, CS):
                     cs = slice(x, x + CS)
                     s = nn(kc, qt[t, :, cs])
+                    if ahead_dp:
+                        dp_s[pl.ds(pos, nb), :, cs] = nn(vc, dt[t, :, cs]).reshape(nb, BLK, CS)
                     for u in range(nb):
                         for q in range(NG):
                             lo = u * BLK + q * MG
@@ -457,17 +460,21 @@
                 return local(body, lax.fori_loop(0, whole, lambda c, x: body(0, PROMPT, False, x), init))
 
             def p1(pos, nb, diag, x):
-                first_pass(pos, nb, diag)
+                first_pass(pos, nb, diag, False)
+                return x
+
+            def p1_both(pos, nb, diag, x):
+                first_pass(pos, nb, diag, True)
                 return x
 
             @pl.when(i == 0)
             def _():
                 local_arrive()
-                local(p1, 0)
+                local(p1_both, 0)
                 chain_arrive()
-                lax.fori_loop(0, whole, lambda c, x: p1(y * CBP, CBP, False, x), 0)
+                lax.fori_loop(0, whole, lambda c, x: p1_both(y * CBP, CBP, False, x), 0)
                 rest_arrive()
-                lax.fori_loop(0, whole, lambda c, x: p1((1 - y) * CBP, CBP, False, x), 0)
+                lax.fori_loop(0, whole, lambda c, x: p1_both((1 - y) * CBP, CBP, False, x), 0)
 
             @pl.when(i > 0)
             def _():
@@ -480,17 +487,17 @@
             m_s[...] = f * (1.0 / tot)[None]
 
             drows = dn[t]
-            def p3(pos, nb, diag, acc):
+            def p3_with(have_dp, pos, nb, acc):
                 r0 = row0(pos)
                 vc = kv_ref[pl.ds(r0, nb * BLK), BLK:2 * BLK]
                 accs, ps = [], []
                 for x in range(0, RT, CS):
                     cs = slice(x, x + CS)
-                    dp = nn(vc, dt[t, :, cs])
+                    dp = None if have_dp else nn(vc, dt[t, :, cs])
                     a = acc[:, cs]
                     pu = []
                     for u in range(nb):
-                        du = dp[u * BLK:(u + 1) * BLK]
+                        du = dp_s[pos + u, :, cs] if have_dp else dp[u * BLK:(u + 1) * BLK]
                         parts = []
                         for q in range(NG):
                             wq = w_s[pos + u, q * MG:(q + 1) * MG, cs].reshape(MG // 8, 8, CS)
@@ -498,7 +505,8 @@
                         ch = jnp.concatenate(parts, axis=0)
                         chb = ch.astype(BF)
                         w_s[pos + u, :, cs] = ch
-                        dp_s[pos + u, :, cs] = du
+                        if not have_dp:
+                            dp_s[pos + u, :, cs] = du
                         a = a + jnp.sum((chb.astype(F32) * du).reshape(BLK // 8, 8, CS), axis=0)
                         pu.append(chb)
                     accs.append(a)
@@ -508,7 +516,15 @@
                 dv_ref[rows, :] += nn(p, drows)
                 return jnp.concatenate(accs, axis=1)
 
-            delta = over(p3, jnp.zeros((8, RT), F32))
+            @pl.when(i == 0)
+            def _():
+                dl_s[...] = over(lambda pos, nb, diag, acc: p3_with(True, pos, nb, acc), jnp.zeros((8, RT), F32))
+
+            @pl.when(i > 0)
+            def _():
+                dl_s[...] = over(lambda pos, nb, diag, acc: p3_with(False, pos, nb, acc), jnp.zeros((8, RT), F32))
+
+            delta = dl_s[...]
             @pl.when(i == 3)
             def _():
                 hand_over(0, 0, OWN)
@@ -751,6 +767,7 @@
             pltpu.VMEM((POS, BLK, RT), F32),
             pltpu.VMEM((POS * NG, 8, RT), F32),
             pltpu.VMEM((POS * NG, 8, RT), F32),
+            pltpu.VMEM((8, RT), F32),
             pltpu.VMEM((tiles, BLK, RT), F32),
             pltpu.VMEM((rows, BLK), F32),
             pltpu.VMEM((rows, BLK), F32),

time: 93.8 us -> 93.3 us (level)
  no operation moved by 1% of the time
where the time goes in v7:
time: 93.3 us; the launch traced here: 93.1 us
  Pallas kernels  92.5 us (99%)
    pallas_call x1, Pallas kernels, fused(): pl.pallas_call(fused_kernel, out_shape=(jax.ShapeDtypeStruct((512, 1024),...  89.2 us
    pallas_call x1, Pallas kernels, hand_out(): pl.pallas_call(hand_out_kernel, out_shape=tuple((jax.ShapeDtypeStruct(t.s...  3.29 us

profile of v7, /device:TPU:1, one launch (start us, length us, event | category | flops | bytes accessed | tf_op | source)
XLA Modules:
  0.0 93.1 jit_solution(8523624390050097438)
XLA Ops:
  0.6 89.2 %shard_map.119 = (bf16[512,1024]{1,0:T(8,128)(2,1)}, bf16[512,128]{1,0:T(8,128)(2,1)}, bf16[512,128]{1,0:T(8,128)(2,1)}, f32[8,128]{1,0:T(8,128)}) custom-call(s32[8]{0:T(128)} %bitcast.15, s32[4]{0:T(128)} %bitcast.16, f32[1,128]{1,0:T(1,128)} %bitcast.17, f32[1,128]{1,0:T(1,128)} %bitcast.18, bf16[512,1024]{1,0:T(8,128)(2,1)} %bitcast.11, ...), custom_call_target="tpu_custom_call" | custom-call | tf_op jit(solution)/shard_map/pallas_call | solution.py:748
  89.8 3.3 %shard_map.120 = (bf16[512,1024]{1,0:T(8,128)(2,1)}, bf16[512,128]{1,0:T(8,128)(2,1)}, bf16[512,128]{1,0:T(8,128)(2,1)}, f32[128]{0:T(128)}, f32[128]{0:T(128)}) custom-call(f32[8,128]{1,0:T(8,128)} %get-tuple-element.14.gains_ref, bf16[512,1024]{1,0:T(8,128)(2,1)} %get-tuple-element.15.gq_ref, bf16[512,128]{1,0:T(8,128)(2,1)} %get-tuple-element.16.gk_ref, ...), custom_call_target="tpu_custom_call" | custom-call | tf_op jit(solution)/shard_map/pallas_call | solution.py:814
